TPU v7x, 32 devices: a whole 2x2x4 slice. The times are simulated.
32 devices in a mesh: dp: 8 (over z, x), fsdp: 4 (over y, core).
Axes of the slice: x: 2, y: 2, z: 4, core: 2. Of those that a mesh axis runs over, the one named last changes fastest.
Arguments:
- block_input: bfloat16 [16384, 1024], P(('dp', 'fsdp')), may hold values from -6 to 6
- out_cotangent: bfloat16 [16384, 1024], P(('dp', 'fsdp')), may hold values from -6 to 6
- inproj: float32 [1024, 3072], P(None, ('dp', 'fsdp')), may hold values from -0.1875 to 0.1875
- convtaps: float32 [3, 1024], P(None, ('dp', 'fsdp')), may hold values from -3.5 to 3.5
- outproj: float32 [1024, 1024], P(None, ('dp', 'fsdp')), may hold values from -0.1875 to 0.1875
- gateproj: float32 [1024, 4608], P(None, ('dp', 'fsdp')), may hold values from -0.1875 to 0.1875
- upproj: float32 [1024, 4608], P(None, ('dp', 'fsdp')), may hold values from -0.1875 to 0.1875
- downproj: float32 [4608, 1024], P(None, ('dp', 'fsdp')), may hold values from -0.1875 to 0.1875
- normgains: float32 [2, 1024], P(None, ('dp', 'fsdp')), may hold values from 0.1 to 1.9
- first_inproj: float32 [1024, 3072], P(None, ('dp', 'fsdp')), may hold values from -128 to 128
- first_convtaps: float32 [3, 1024], P(None, ('dp', 'fsdp')), may hold values from -128 to 128
- first_outproj: float32 [1024, 1024], P(None, ('dp', 'fsdp')), may hold values from -128 to 128
- first_gateproj: float32 [1024, 4608], P(None, ('dp', 'fsdp')), may hold values from -40 to 40
- first_upproj: float32 [1024, 4608], P(None, ('dp', 'fsdp')), may hold values from -40 to 40
- first_downproj: float32 [4608, 1024], P(None, ('dp', 'fsdp')), may hold values from -40 to 40
- first_normgains: float32 [2, 1024], P(None, ('dp', 'fsdp')), may hold values from -160 to 160
- second_inproj: float32 [1024, 3072], P(None, ('dp', 'fsdp')), may hold values from 58.9824 to 235.9296
- second_convtaps: float32 [3, 1024], P(None, ('dp', 'fsdp')), may hold values from 58.9824 to 235.9296
- second_outproj: float32 [1024, 1024], P(None, ('dp', 'fsdp')), may hold values from 58.9824 to 235.9296
- second_gateproj: float32 [1024, 4608], P(None, ('dp', 'fsdp')), may hold values from 4.58752 to 18.35008
- second_upproj: float32 [1024, 4608], P(None, ('dp', 'fsdp')), may hold values from 4.9152 to 19.6608
- second_downproj: float32 [4608, 1024], P(None, ('dp', 'fsdp')), may hold values from 4.096 to 16.384
- second_normgains: float32 [2, 1024], P(None, ('dp', 'fsdp')), may hold values from 81.92 to 327.68
Outputs:
- block_output: bfloat16 [16384, 1024], P(('dp', 'fsdp'))
- input_grad: float32 [16384, 1024], P(('dp', 'fsdp'))
- moment_inproj: float32 [1024, 3072], P(None, ('dp', 'fsdp'))
- square_inproj: float32 [1024, 3072], P(None, ('dp', 'fsdp'))
- weight_inproj: float32 [1024, 3072], P(None, ('dp', 'fsdp'))
- moment_convtaps: float32 [3, 1024], P(None, ('dp', 'fsdp'))
- square_convtaps: float32 [3, 1024], P(None, ('dp', 'fsdp'))
- weight_convtaps: float32 [3, 1024], P(None, ('dp', 'fsdp'))
- moment_outproj: float32 [1024, 1024], P(None, ('dp', 'fsdp'))
- square_outproj: float32 [1024, 1024], P(None, ('dp', 'fsdp'))
- weight_outproj: float32 [1024, 1024], P(None, ('dp', 'fsdp'))
- moment_gateproj: float32 [1024, 4608], P(None, ('dp', 'fsdp'))
- square_gateproj: float32 [1024, 4608], P(None, ('dp', 'fsdp'))
- weight_gateproj: float32 [1024, 4608], P(None, ('dp', 'fsdp'))
- moment_upproj: float32 [1024, 4608], P(None, ('dp', 'fsdp'))
- square_upproj: float32 [1024, 4608], P(None, ('dp', 'fsdp'))
- weight_upproj: float32 [1024, 4608], P(None, ('dp', 'fsdp'))
- moment_downproj: float32 [4608, 1024], P(None, ('dp', 'fsdp'))
- square_downproj: float32 [4608, 1024], P(None, ('dp', 'fsdp'))
- weight_downproj: float32 [4608, 1024], P(None, ('dp', 'fsdp'))
- moment_normgains: float32 [2, 1024], P(None, ('dp', 'fsdp'))
- square_normgains: float32 [2, 1024], P(None, ('dp', 'fsdp'))
- weight_normgains: float32 [2, 1024], P(None, ('dp', 'fsdp'))
All inputs are finite; a program needn't handle non-finite values.
Results may differ from a plain program's by a relative error of at most 0.012.
The roundings to bfloat16 on the way count: a program that leaves them out, or rounds other values in their place, can miss the bound.
Values may be sent and summed in bfloat16 or wider, within the bound.
A program may use at most 384 MiB of HBM per device.

v0:
```python
import jax
import jax.numpy as jnp
from jax import lax
from jax.sharding import PartitionSpec as P

KERNEL = 3
SEQ = 512
STEP = 10


eps_norm = 1e-05
beta_one = 0.9
beta_two = 0.999
eps_adam = 1e-08
rates = (0.06, 0.5, 0.06, 0.06, 0.06, 0.06, 0.5)
decays = (0.01, 0.01, 0.01, 0.01, 0.01, 0.01, 0.0)


def norm_rows(values, gain):
    return values * lax.rsqrt(jnp.mean(values * values, axis=-1, keepdims=True) + eps_norm) * gain


def mix_conv(projected, filters):
    width = filters.shape[1]
    seqcount = projected.shape[0] // SEQ
    gated = projected[:, :width] * projected[:, 2 * width :]
    blocks = gated.reshape(seqcount, SEQ, width)
    padded = jnp.pad(blocks, ((0, 0), (KERNEL - 1, 0), (0, 0)))
    mixed = filters[0] * padded[:, 0:SEQ]
    for offset in range(1, KERNEL):
        mixed = mixed + filters[offset] * padded[:, offset : offset + SEQ]
    return projected[:, width : 2 * width] * mixed.reshape(-1, width)


def swiglu(gate, upward):
    return jax.nn.silu(gate) * upward


def adamw_step(param, grad, first, second, rate, decay):
    moment = beta_one * first + (1.0 - beta_one) * grad
    square = beta_two * second + (1.0 - beta_two) * grad * grad
    mhat = moment / (1.0 - beta_one**STEP)
    vhat = square / (1.0 - beta_two**STEP)
    updated = param - rate * (mhat / (jnp.sqrt(vhat) + eps_adam) + decay * param)
    return (moment, square, updated)


def pack_owners(grads, owners):
    pieces = []
    for grad in grads:
        rows, cols = grad.shape
        share = cols // owners
        pieces.append(
            grad.reshape(rows, owners, share).transpose(1, 0, 2).reshape(owners, rows * share)
        )
    return jnp.concatenate(pieces, axis=1)


def unpack_owned(flat_row, grads, owners):
    results = []
    offset = 0
    for grad in grads:
        rows, cols = grad.shape
        share = cols // owners
        length = rows * share
        results.append(flat_row[0, offset : offset + length].reshape(rows, share))
        offset = offset + length
    return tuple(results)


def shards(
    block_input,
    out_cotangent,
    inproj,
    convtaps,
    outproj,
    gateproj,
    upproj,
    downproj,
    normgains,
    first_inproj,
    first_convtaps,
    first_outproj,
    first_gateproj,
    first_upproj,
    first_downproj,
    first_normgains,
    second_inproj,
    second_convtaps,
    second_outproj,
    second_gateproj,
    second_upproj,
    second_downproj,
    second_normgains,
):
    masters = (inproj, convtaps, outproj, gateproj, upproj, downproj, normgains)
    firsts = (
        first_inproj,
        first_convtaps,
        first_outproj,
        first_gateproj,
        first_upproj,
        first_downproj,
        first_normgains,
    )
    seconds = (
        second_inproj,
        second_convtaps,
        second_outproj,
        second_gateproj,
        second_upproj,
        second_downproj,
        second_normgains,
    )
    halves = tuple((item.astype(jnp.bfloat16) for item in masters))
    gathered = (
        lax.all_gather(halves[0], ("dp", "fsdp"), axis=1, tiled=True),
        lax.all_gather(halves[1], ("dp", "fsdp"), axis=1, tiled=True),
        lax.all_gather(halves[2], ("dp", "fsdp"), axis=1, tiled=True),
        lax.all_gather(halves[3], ("dp", "fsdp"), axis=1, tiled=True),
        lax.all_gather(halves[4], ("dp", "fsdp"), axis=1, tiled=True),
        lax.all_gather(halves[5], ("dp", "fsdp"), axis=1, tiled=True),
        lax.all_gather(halves[6], ("dp", "fsdp"), axis=1, tiled=True),
    )
    in_weight, filter_half, out_weight, gate_weight, up_weight, down_weight, gains_half = gathered
    filters = filter_half.astype(jnp.float32)
    gain_one = gains_half[0].astype(jnp.float32)
    gain_two = gains_half[1].astype(jnp.float32)
    resid = block_input.astype(jnp.float32)
    normed = norm_rows(resid, gain_one).astype(jnp.bfloat16)
    projected = jnp.dot(normed, in_weight, preferred_element_type=jnp.float32)
    mixed = mix_conv(projected, filters).astype(jnp.bfloat16)
    middle = resid + jnp.dot(mixed, out_weight, preferred_element_type=jnp.float32)
    normed_two = norm_rows(middle, gain_two).astype(jnp.bfloat16)
    gate = jnp.dot(normed_two, gate_weight, preferred_element_type=jnp.float32)
    upward = jnp.dot(normed_two, up_weight, preferred_element_type=jnp.float32)
    hidden = swiglu(gate, upward).astype(jnp.bfloat16)
    ffn_out = jnp.dot(hidden, down_weight, preferred_element_type=jnp.float32)
    block_output = (middle + ffn_out).astype(jnp.bfloat16)
    again = (
        lax.all_gather(halves[0], ("dp", "fsdp"), axis=1, tiled=True),
        lax.all_gather(halves[1], ("dp", "fsdp"), axis=1, tiled=True),
        lax.all_gather(halves[2], ("dp", "fsdp"), axis=1, tiled=True),
        lax.all_gather(halves[3], ("dp", "fsdp"), axis=1, tiled=True),
        lax.all_gather(halves[4], ("dp", "fsdp"), axis=1, tiled=True),
        lax.all_gather(halves[5], ("dp", "fsdp"), axis=1, tiled=True),
        lax.all_gather(halves[6], ("dp", "fsdp"), axis=1, tiled=True),
    )
    in_weight, filter_half, out_weight, gate_weight, up_weight, down_weight, gains_half = again
    filters = filter_half.astype(jnp.float32)
    gain_one = gains_half[0].astype(jnp.float32)
    gain_two = gains_half[1].astype(jnp.float32)
    cotan = out_cotangent.astype(jnp.float32)
    grad_down = jnp.einsum("tf,td->fd", hidden, out_cotangent, preferred_element_type=jnp.float32)
    d_hidden = jnp.einsum(
        "td,fd->tf", out_cotangent, down_weight, preferred_element_type=jnp.float32
    )
    unused_value, swiglu_back = jax.vjp(swiglu, gate, upward)
    d_gate, d_upward = swiglu_back(d_hidden)
    d_gate = d_gate.astype(jnp.bfloat16)
    d_upward = d_upward.astype(jnp.bfloat16)
    grad_gate = jnp.einsum("td,tf->df", normed_two, d_gate, preferred_element_type=jnp.float32)
    grad_up = jnp.einsum("td,tf->df", normed_two, d_upward, preferred_element_type=jnp.float32)
    d_normed_two = jnp.einsum(
        "tf,df->td", d_gate, gate_weight, preferred_element_type=jnp.float32
    ) + jnp.einsum("tf,df->td", d_upward, up_weight, preferred_element_type=jnp.float32)
    unused_two, norm_back_two = jax.vjp(norm_rows, middle, gain_two)
    d_middle_norm, grad_gain_two = norm_back_two(d_normed_two)
    d_middle = cotan + d_middle_norm
    d_branch = d_middle.astype(jnp.bfloat16)
    grad_out = jnp.einsum("td,te->de", mixed, d_branch, preferred_element_type=jnp.float32)
    d_mixed = jnp.einsum("te,de->td", d_branch, out_weight, preferred_element_type=jnp.float32)
    unused_three, conv_back = jax.vjp(mix_conv, projected, filters)
    d_projected, grad_filters = conv_back(d_mixed)
    d_projected = d_projected.astype(jnp.bfloat16)
    grad_in = jnp.einsum("td,te->de", normed, d_projected, preferred_element_type=jnp.float32)
    d_normed = jnp.einsum("te,de->td", d_projected, in_weight, preferred_element_type=jnp.float32)
    unused_four, norm_back_one = jax.vjp(norm_rows, resid, gain_one)
    d_resid_norm, grad_gain_one = norm_back_one(d_normed)
    input_grad = d_middle + d_resid_norm
    grad_gains = jnp.stack([grad_gain_one, grad_gain_two])
    owners = lax.axis_size(("dp", "fsdp"))
    full_grads = (grad_in, grad_filters, grad_out, grad_gate, grad_up, grad_down, grad_gains)
    packed = pack_owners(full_grads, owners)
    own_row = lax.psum_scatter(packed, ("dp", "fsdp"), scatter_dimension=0, tiled=True)
    owned = unpack_owned(own_row, full_grads, owners)
    outputs = [block_output, input_grad]
    for position in range(7):
        moment, square, updated = adamw_step(
            masters[position],
            owned[position],
            firsts[position],
            seconds[position],
            rates[position],
            decays[position],
        )
        outputs = outputs + [moment, square, updated]
    return tuple(outputs)


def solution(mesh):
    return jax.shard_map(
        shards,
        mesh=mesh,
        in_specs=(
            P(("dp", "fsdp"), None),
            P(("dp", "fsdp"), None),
            P(None, ("dp", "fsdp")),
            P(None, ("dp", "fsdp")),
            P(None, ("dp", "fsdp")),
            P(None, ("dp", "fsdp")),
            P(None, ("dp", "fsdp")),
            P(None, ("dp", "fsdp")),
            P(None, ("dp", "fsdp")),
            P(None, ("dp", "fsdp")),
            P(None, ("dp", "fsdp")),
            P(None, ("dp", "fsdp")),
            P(None, ("dp", "fsdp")),
            P(None, ("dp", "fsdp")),
            P(None, ("dp", "fsdp")),
            P(None, ("dp", "fsdp")),
            P(None, ("dp", "fsdp")),
            P(None, ("dp", "fsdp")),
            P(None, ("dp", "fsdp")),
            P(None, ("dp", "fsdp")),
            P(None, ("dp", "fsdp")),
            P(None, ("dp", "fsdp")),
            P(None, ("dp", "fsdp")),
        ),
        out_specs=(
            P(("dp", "fsdp"), None),
            P(("dp", "fsdp"), None),
            P(None, ("dp", "fsdp")),
            P(None, ("dp", "fsdp")),
            P(None, ("dp", "fsdp")),
            P(None, ("dp", "fsdp")),
            P(None, ("dp", "fsdp")),
            P(None, ("dp", "fsdp")),
            P(None, ("dp", "fsdp")),
            P(None, ("dp", "fsdp")),
            P(None, ("dp", "fsdp")),
            P(None, ("dp", "fsdp")),
            P(None, ("dp", "fsdp")),
            P(None, ("dp", "fsdp")),
            P(None, ("dp", "fsdp")),
            P(None, ("dp", "fsdp")),
            P(None, ("dp", "fsdp")),
            P(None, ("dp", "fsdp")),
            P(None, ("dp", "fsdp")),
            P(None, ("dp", "fsdp")),
            P(None, ("dp", "fsdp")),
            P(None, ("dp", "fsdp")),
            P(None, ("dp", "fsdp")),
        ),
        check_vma=False,
    )
```

profile of v0, /device:TPU:0, one launch (start us, length us, event | category | flops | bytes accessed | tf_op | source)
XLA Modules:
  0.0 2105.1 jit_solution(2597073201989020773)
XLA Ops:
  14.4 43.1 %all-gather = bf16[32,32,2]{1,2,0:T(2,128)(2,1)S(1)} all-gather(bf16[1,32,2]{1,2,0:T(2,128)(2,1)S(1)} %convert_bitcast_fusion.1), channel_id=1, replica_groups=mesh['dp'=8,'fsdp'=4] {'dp','fsdp'}, dimensions={0}, use_global_device_ids=true | all-gather | bytes 4224 | tf_op jit(solution)/shard_map/all_gather | solution.py:123
  57.6 36.8 %all-gather.1 = bf16[32,32,3]{1,2,0:T(4,128)(2,1)S(1)} all-gather(bf16[1,32,3]{1,2,0:T(4,128)(2,1)S(1)} %convert_bitcast_fusion), channel_id=1, replica_groups=mesh['dp'=8,'fsdp'=4] {'dp','fsdp'}, dimensions={0}, use_global_device_ids=true | all-gather | bytes 6336 | tf_op jit(solution)/shard_map/all_gather | solution.py:118
  95.4 5.8 fusion.26
  101.6 2.2 copy-done
  103.7 2.4 fusion.15
  106.1 36.1 %all-gather.10.cloned.1.call-done = bf16[1024,1024]{0,1:T(8,128)(2,1)} async-done(((bf16[1024,32]{0,1:T(8,128)(2,1)}), bf16[1024,1024]{0,1:T(8,128)(2,1)}) %all-gather.10.cloned.1.call-update) | async-done | bytes 2097168 | tf_op jit(solution)/shard_map/all_gather | solution.py:119
  142.3 3.2 multiply_reduce_fusion.3
  148.1 78.6 %all-gather.12.cloned.1.call-done = bf16[1024,4608]{0,1:T(8,128)(2,1)} async-done(((bf16[1024,144]{0,1:T(8,128)(2,1)}), bf16[1024,4608]{0,1:T(8,128)(2,1)}) %all-gather.12.cloned.1.call-update) | async-done | bytes 9437200 | tf_op jit(solution)/shard_map/all_gather | solution.py:120
  226.7 10.2 fusion.43
  236.9 73.8 %all-gather.14.cloned.1.call-done = bf16[1024,4608]{0,1:T(8,128)(2,1)} async-done(((bf16[1024,144]{0,1:T(8,128)(2,1)}), bf16[1024,4608]{0,1:T(8,128)(2,1)}) %all-gather.14.cloned.1.call-update) | async-done | bytes 9437200 | tf_op jit(solution)/shard_map/all_gather | solution.py:121
  310.7 10.2 fusion.44
  320.9 73.8 %all-gather.16.cloned.1.call-done = bf16[4608,1024]{0,1:T(8,128)(2,1)} async-done(((bf16[4608,32]{0,1:T(8,128)(2,1)}), bf16[4608,1024]{0,1:T(8,128)(2,1)}) %all-gather.16.cloned.1.call-update) | async-done | bytes 9437200 | tf_op jit(solution)/shard_map/all_gather | solution.py:122
  394.7 28.2 %multiply_convert_fusion = (bf16[512,4608]{1,0:T(8,128)(2,1)}, bf16[512,4608]{1,0:T(8,128)(2,1)}, bf16[512,4608]{1,0:T(8,128)(2,1)}) fusion(f32[512,4608]{1,0:T(8,128)} %fusion.43, f32[512,4608]{1,0:T(8,128)} %fusion.44, bf16[512,1024]{1,0:T(8,128)(2,1)} %param.24, bf16[4608,1024]{0,1:T(8,128)(2,1)} %all-gather.16.cloned.1.call-done), kind=kOutput, calls=%fused_computation.4 | convolution fusion | flops 4869586944 | bytes 43515904 | tf_op jit(solution)/shard_map/td,fd->tf/dot_general | solution.py:155
  422.9 9.1 fusion.45
  432.7 5.9 multiply_reduce_fusion
  444.8 3.3 fusion.20
  448.1 11.6 fusion.46
  459.6 9.5 fusion.47
  471.0 7.1 fusion.24
  478.1 15.5 copy.147
  493.6 14.5 reshape.178
  508.1 10.0 constant_dynamic-update-slice_fusion
  518.4 10.5 copy.149
  528.8 11.8 reshape.183
  540.6 26.4 %copy.151 = f32[32,1024,144]{2,1,0:T(8,128)} copy(f32[32,1024,144]{1,2,0:T(8,128)} %bitcast.96) | data formatting | bytes 37748736 | tf_op jit(solution)/shard_map/transpose | solution.py:54
  567.1 54.0 %reshape.185 = f32[32,147456]{1,0:T(8,128)} reshape(f32[32,1024,144]{2,1,0:T(8,128)} %copy.151) | data formatting | bytes 37748736 | tf_op jit(solution)/shard_map/reshape | solution.py:54
  621.1 26.4 %copy.153 = f32[32,1024,144]{2,1,0:T(8,128)} copy(f32[32,1024,144]{1,2,0:T(8,128)} %bitcast.95) | data formatting | bytes 37748736 | tf_op jit(solution)/shard_map/transpose | solution.py:54
  647.5 54.6 %reshape.187 = f32[32,147456]{1,0:T(8,128)} reshape(f32[32,1024,144]{2,1,0:T(8,128)} %copy.153) | data formatting | bytes 37748736 | tf_op jit(solution)/shard_map/reshape | solution.py:54
  702.1 11.3 fusion.48
  713.4 40.1 %copy.154 = f32[4608,32,32]{2,0,1:T(8,128)} copy(f32[4608,32,32]{0,2,1:T(8,128)} %bitcast.97) | data formatting | bytes 37748736 | tf_op jit(solution)/shard_map/reshape | solution.py:54
  753.5 68.0 %reshape.189 = f32[32,147456]{1,0:T(8,128)} reshape(f32[32,4608,32]{2,1,0:T(8,128)} %bitcast.32) | data formatting | bytes 37748736 | tf_op jit(solution)/shard_map/reshape | solution.py:54
  821.7 9.0 fusion.7
  832.3 15.0 dynamic-update-slice.2
  847.3 53.7 %dynamic-update-slice.3 = f32[32,573600]{1,0:T(8,128)} dynamic-update-slice(f32[32,573600]{1,0:T(8,128)} %dynamic-update-slice.2, f32[32,147456]{1,0:T(8,128)} %reshape.185, s32[]{} %constant.142, s32[]{} %constant.145) | dynamic-update-slice | bytes 37748740
  901.1 53.7 %dynamic-update-slice.4 = f32[32,573600]{1,0:T(8,128)} dynamic-update-slice(f32[32,573600]{1,0:T(8,128)} %dynamic-update-slice.3, f32[32,147456]{1,0:T(8,128)} %reshape.187, s32[]{} %constant.142, s32[]{} %constant.146) | dynamic-update-slice | bytes 37748740
  954.8 53.2 %dynamic-update-slice.5 = f32[32,573600]{1,0:T(8,128)} dynamic-update-slice(f32[32,573600]{1,0:T(8,128)} %dynamic-update-slice.4, f32[32,147456]{1,0:T(8,128)} %reshape.189, s32[]{} %constant.142, s32[]{} %constant.147) | dynamic-update-slice | bytes 37748740
  1011.5 2.0 copy.155
  1013.5 2.1 copy.145
  1015.6 3.6 fusion.9
  1019.2 10.2 add_convert_fusion.1
  1029.4 1031.5 %all-reduce.13.cloned.1.call-done = f32[32,573600]{1,0:T(8,128)} async-done(((f32[32,573600]{1,0:T(8,128)}), f32[32,573600]{1,0:T(8,128)}) %all-reduce.13.cloned.1.call-update) | async-done | bytes 73420816
  2060.9 2.9 dynamic-slice_reduce_fusion.3
  2065.2 2.0 copy.170
  2072.6 10.3 dynamic-slice_reduce_fusion
  2084.9 1.9 reshape_squeeze.26
  2089.8 1.9 multiply_subtract_fusion.4
  2091.7 3.2 multiply_subtract_fusion
  2095.6 2.4 multiply_subtract_fusion.1
  (170 shorter events, 37.2 us)
Async XLA Ops:
  7.2 5.5 copy-start.11
  7.2 6.4 copy-start.13
  7.2 87.7 %all-gather.8.cloned.1.call-start = ((), (), s32[]{:S(2)}) async-start(), calls=%async_computation | async-start | bytes 6488064 | tf_op jit(solution)/shard_map/all_gather | solution.py:117
  9.0 5.3 copy-start.41
  9.0 48.5 %copy-start.36 = (f32[3,32]{1,0:T(4,128)S(1)}, f32[3,32]{1,0:T(4,128)}, u32[]{:S(2)}) copy-start(f32[3,32]{1,0:T(4,128)} %param.26) | copy-start | bytes 1156
  9.0 85.4 %copy-start.7 = (bf16[512,1024]{1,0:T(8,128)(2,1)S(1)}, bf16[512,1024]{1,0:T(8,128)(2,1)}, u32[]{:S(2)}) copy-start(bf16[512,1024]{1,0:T(8,128)(2,1)} %param.23) | copy-start | bytes 3145732
  9.1 133.2 %all-gather.10.cloned.1.call-start = ((), (), s32[]{:S(2)}) async-start(), calls=%async_computation.1 | async-start | bytes 2162688 | tf_op jit(solution)/shard_map/all_gather | solution.py:119
  10.8 215.9 %all-gather.12.cloned.1.call-start = ((), (), s32[]{:S(2)}) async-start(), calls=%async_computation.2 | async-start | bytes 9732096 | tf_op jit(solution)/shard_map/all_gather | solution.py:120
  12.7 298.1 %all-gather.14.cloned.1.call-start = ((), (), s32[]{:S(2)}) async-start(), calls=%async_computation.3 | async-start | bytes 9732096 | tf_op jit(solution)/shard_map/all_gather | solution.py:121
  13.5 381.2 %all-gather.16.cloned.1.call-start = ((), (), s32[]{:S(2)}) async-start(), calls=%async_computation.4 | async-start | bytes 9732096 | tf_op jit(solution)/shard_map/all_gather | solution.py:122
  14.3 2046.6 %all-reduce.13.cloned.1.call-start = ((), (), s32[]{:S(2)}) async-start(), calls=%async_computation.5 | async-start | bytes 146866176
  94.8 376.1 %copy-start.34 = (f32[512]{0:T(512)}, f32[512]{0:T(512)S(1)}, u32[]{:S(2)}) copy-start(f32[512]{0:T(512)S(1)} %fusion.30) | copy-start | bytes 6148
  94.8 376.1 %copy-start.32 = (f32[1,1024]{1,0:T(1,128)}, f32[1,1024]{1,0:T(1,128)S(1)}, u32[]{:S(2)}) copy-start(f32[1,1024]{1,0:T(1,128)S(1)} %get-tuple-element.139) | copy-start | bytes 12292
  422.9 9.2 copy-start.4
  422.9 9.2 copy-start.45
  422.9 9.8 copy-start.46
  422.9 16.3 slice-start
  432.7 5.9 copy-start.24
  432.7 6.6 slice-start.1
  438.6 3.0 copy-start.20
  439.2 5.5 copy-start.1
  443.2 27.8 %copy-start.21 = (f32[512,1024]{1,0:T(8,128)}, f32[512,1024]{1,0:T(8,128)S(1)}, u32[]{:S(2)}) copy-start(f32[512,1024]{1,0:T(8,128)S(1)} %get-tuple-element.131) | copy-start | bytes 6291460
  444.8 3.3 copy-start.23
  444.8 14.9 slice-start.2
  448.1 11.6 slice-start.3
  470.9 7.2 copy-start.14
  470.9 7.2 copy-start.16
  647.5 54.6 %copy-start.25 = (bf16[512,1024]{1,0:T(8,128)(2,1)S(1)}, bf16[512,1024]{1,0:T(8,128)(2,1)}, u32[]{:S(2)}) copy-start(bf16[512,1024]{1,0:T(8,128)(2,1)} %param.24) | copy-start | bytes 3145732
  753.5 68.1 %copy-start.38 = (f32[1024]{0:T(1024)S(1)}, f32[1024]{0:T(1024)}, u32[]{:S(2)}) copy-start(f32[1024]{0:T(1024)} %get-tuple-element.95) | copy-start | bytes 12292
  753.5 68.1 %copy-start.9 = (bf16[512,1024]{1,0:T(8,128)(2,1)S(1)}, bf16[512,1024]{1,0:T(8,128)(2,1)}, u32[]{:S(2)}) copy-start(bf16[512,1024]{1,0:T(8,128)(2,1)} %param.23) | copy-start | bytes 3145732
  753.5 68.2 %copy-start.15 = (f32[512,1024]{1,0:T(8,128)S(1)}, f32[512,1024]{1,0:T(8,128)}, u32[]{:S(2)}) copy-start(f32[512,1024]{1,0:T(8,128)} %copy-done.14) | copy-start | bytes 6291460
  753.5 68.2 %copy-start.33 = (f32[1,1024]{1,0:T(1,128)S(1)}, f32[1,1024]{1,0:T(1,128)}, u32[]{:S(2)}) copy-start(f32[1,1024]{1,0:T(1,128)} %copy-done.32) | copy-start | bytes 12292
  753.5 68.2 %copy-start.35 = (f32[512]{0:T(512)S(1)}, f32[512]{0:T(512)}, u32[]{:S(2)}) copy-start(f32[512]{0:T(512)} %copy-done.34) | copy-start | bytes 6148
  1010.5 5.1 copy-start.31
  1010.5 5.1 copy-start.2
  1015.6 3.6 copy-start.5
  1019.2 1044.8 %copy-start.17 = (f32[1024,96]{1,0:T(8,128)S(1)}, f32[1024,96]{1,0:T(8,128)}, u32[]{:S(2)}) copy-start(f32[1024,96]{1,0:T(8,128)} %copy.157) | copy-start | bytes 1179652
  1019.2 1044.8 %copy-start.18 = (f32[1024,96]{1,0:T(8,128)S(1)}, f32[1024,96]{1,0:T(8,128)}, u32[]{:S(2)}) copy-start(f32[1024,96]{1,0:T(8,128)} %copy.155) | copy-start | bytes 1179652
  1019.2 1044.8 %copy-start.19 = (f32[1024,96]{1,0:T(8,128)S(1)}, f32[1024,96]{1,0:T(8,128)}, u32[]{:S(2)}) copy-start(f32[1024,96]{1,0:T(8,128)} %copy.145) | copy-start | bytes 1179652
  2091.6 3.3 copy-start.42
  2091.6 3.3 copy-start.43
  2091.6 3.3 copy-start.44
  2091.7 3.9 copy-start.10
  2091.7 3.9 copy-start.12
  2091.7 3.9 copy-start.26
  2091.7 3.9 copy-start.27
  2091.7 3.9 copy-start.28
  2091.7 3.9 copy-start.29
  (9 other events, 16.0 us)
Sparse Core Ops, SparseCore 0:
  11.5 72.3 all-gather.7
  87.4 54.8 all-gather.9
  145.8 80.8 all-gather.11
  230.0 80.6 all-gather.13
  314.1 80.6 all-gather.15
  1009.6 1051.2 all-reduce.12
where the time goes:
time: 2120 us; the launch traced here: 2110 us
  waiting for transfers between devices  1290 us (61%)
  local copies, waits for them, and re-layouts  551 us (26%)
  matrix products  136 us (6%)
  blocking collectives  79.9 us (4%)
  other arithmetic  28.5 us (1%)
    unnamed x7, waiting for transfers between devices  1030 us
    reshape x10, local copies, waits for them, and re-layouts, pack_owners(): grad.reshape(rows, owners, share).transpose(1, 0, 2)  254 us
    unnamed x115, local copies, waits for them, and re-layouts  204 us
    all_gather x1, waiting for transfers between devices, shards(): lax.all_gather(halves[3], ('dp', 'fsdp'), axis=1, tiled=True)  78.6 us
    all_gather x1, waiting for transfers between devices, shards(): lax.all_gather(halves[5], ('dp', 'fsdp'), axis=1, tiled=True)  73.8 us
    all_gather x1, waiting for transfers between devices, shards(): lax.all_gather(halves[4], ('dp', 'fsdp'), axis=1, tiled=True)  73.8 us
    transpose x4, local copies, waits for them, and re-layouts, pack_owners(): grad.reshape(rows, owners, share).transpose(1, 0, 2)  68.4 us
    all_gather x1, blocking collectives, shards(): lax.all_gather(halves[6], ('dp', 'fsdp'), axis=1, tiled=True)  43.1 us
  transfers between devices with their start and end apart: 6, of which 5 were waited for; matrix products, arithmetic and copies ran while one was open for 3% of the time, Pallas kernels for 0%

commit v1 on v0

--- a/solution.py
+++ b/solution.py
@@ -43,29 +43,6 @@
     vhat = square / (1.0 - beta_two**STEP)
     updated = param - rate * (mhat / (jnp.sqrt(vhat) + eps_adam) + decay * param)
     return (moment, square, updated)
-
-
-def pack_owners(grads, owners):
-    pieces = []
-    for grad in grads:
-        rows, cols = grad.shape
-        share = cols // owners
-        pieces.append(
-            grad.reshape(rows, owners, share).transpose(1, 0, 2).reshape(owners, rows * share)
-        )
-    return jnp.concatenate(pieces, axis=1)
-
-
-def unpack_owned(flat_row, grads, owners):
-    results = []
-    offset = 0
-    for grad in grads:
-        rows, cols = grad.shape
-        share = cols // owners
-        length = rows * share
-        results.append(flat_row[0, offset : offset + length].reshape(rows, share))
-        offset = offset + length
-    return tuple(results)
 
 
 def shards(
@@ -112,78 +89,77 @@
         second_downproj,
         second_normgains,
     )
-    halves = tuple((item.astype(jnp.bfloat16) for item in masters))
-    gathered = (
-        lax.all_gather(halves[0], ("dp", "fsdp"), axis=1, tiled=True),
-        lax.all_gather(halves[1], ("dp", "fsdp"), axis=1, tiled=True),
-        lax.all_gather(halves[2], ("dp", "fsdp"), axis=1, tiled=True),
-        lax.all_gather(halves[3], ("dp", "fsdp"), axis=1, tiled=True),
-        lax.all_gather(halves[4], ("dp", "fsdp"), axis=1, tiled=True),
-        lax.all_gather(halves[5], ("dp", "fsdp"), axis=1, tiled=True),
-        lax.all_gather(halves[6], ("dp", "fsdp"), axis=1, tiled=True),
-    )
-    in_weight, filter_half, out_weight, gate_weight, up_weight, down_weight, gains_half = gathered
-    filters = filter_half.astype(jnp.float32)
-    gain_one = gains_half[0].astype(jnp.float32)
-    gain_two = gains_half[1].astype(jnp.float32)
+    shard_axes = ("dp", "fsdp")
+    in_weight, out_weight, gate_weight, up_weight, down_weight = (
+        lax.all_gather(item.astype(jnp.bfloat16).T, shard_axes, axis=0, tiled=True)
+        for item in (inproj, outproj, gateproj, upproj, downproj)
+    )
+    small = jnp.concatenate([convtaps, normgains], axis=0).astype(jnp.bfloat16)
+    small = lax.all_gather(small, shard_axes, axis=1, tiled=True).astype(jnp.float32)
+    filters = small[:KERNEL]
+    gain_one = small[KERNEL]
+    gain_two = small[KERNEL + 1]
     resid = block_input.astype(jnp.float32)
     normed = norm_rows(resid, gain_one).astype(jnp.bfloat16)
-    projected = jnp.dot(normed, in_weight, preferred_element_type=jnp.float32)
+    projected = jnp.einsum("td,ed->te", normed, in_weight, preferred_element_type=jnp.float32)
     mixed = mix_conv(projected, filters).astype(jnp.bfloat16)
-    middle = resid + jnp.dot(mixed, out_weight, preferred_element_type=jnp.float32)
+    middle = resid + jnp.einsum("td,ed->te", mixed, out_weight, preferred_element_type=jnp.float32)
     normed_two = norm_rows(middle, gain_two).astype(jnp.bfloat16)
-    gate = jnp.dot(normed_two, gate_weight, preferred_element_type=jnp.float32)
-    upward = jnp.dot(normed_two, up_weight, preferred_element_type=jnp.float32)
+    gate = jnp.einsum("td,fd->tf", normed_two, gate_weight, preferred_element_type=jnp.float32)
+    upward = jnp.einsum("td,fd->tf", normed_two, up_weight, preferred_element_type=jnp.float32)
     hidden = swiglu(gate, upward).astype(jnp.bfloat16)
-    ffn_out = jnp.dot(hidden, down_weight, preferred_element_type=jnp.float32)
+    ffn_out = jnp.einsum("tf,df->td", hidden, down_weight, preferred_element_type=jnp.float32)
     block_output = (middle + ffn_out).astype(jnp.bfloat16)
-    again = (
-        lax.all_gather(halves[0], ("dp", "fsdp"), axis=1, tiled=True),
-        lax.all_gather(halves[1], ("dp", "fsdp"), axis=1, tiled=True),
-        lax.all_gather(halves[2], ("dp", "fsdp"), axis=1, tiled=True),
-        lax.all_gather(halves[3], ("dp", "fsdp"), axis=1, tiled=True),
-        lax.all_gather(halves[4], ("dp", "fsdp"), axis=1, tiled=True),
-        lax.all_gather(halves[5], ("dp", "fsdp"), axis=1, tiled=True),
-        lax.all_gather(halves[6], ("dp", "fsdp"), axis=1, tiled=True),
-    )
-    in_weight, filter_half, out_weight, gate_weight, up_weight, down_weight, gains_half = again
-    filters = filter_half.astype(jnp.float32)
-    gain_one = gains_half[0].astype(jnp.float32)
-    gain_two = gains_half[1].astype(jnp.float32)
     cotan = out_cotangent.astype(jnp.float32)
-    grad_down = jnp.einsum("tf,td->fd", hidden, out_cotangent, preferred_element_type=jnp.float32)
+
+    def owned_sum(left, right):
+        part = jnp.einsum("te,td->ed", left, right, preferred_element_type=jnp.float32)
+        part = part.astype(jnp.bfloat16)
+        total = lax.psum_scatter(part, shard_axes, scatter_dimension=0, tiled=True)
+        return total.astype(jnp.float32).T
+
+    grad_down = owned_sum(out_cotangent, hidden)
     d_hidden = jnp.einsum(
-        "td,fd->tf", out_cotangent, down_weight, preferred_element_type=jnp.float32
+        "td,df->tf", out_cotangent, down_weight, preferred_element_type=jnp.float32
     )
     unused_value, swiglu_back = jax.vjp(swiglu, gate, upward)
     d_gate, d_upward = swiglu_back(d_hidden)
     d_gate = d_gate.astype(jnp.bfloat16)
     d_upward = d_upward.astype(jnp.bfloat16)
-    grad_gate = jnp.einsum("td,tf->df", normed_two, d_gate, preferred_element_type=jnp.float32)
-    grad_up = jnp.einsum("td,tf->df", normed_two, d_upward, preferred_element_type=jnp.float32)
+    grad_gate = owned_sum(d_gate, normed_two)
+    grad_up = owned_sum(d_upward, normed_two)
     d_normed_two = jnp.einsum(
-        "tf,df->td", d_gate, gate_weight, preferred_element_type=jnp.float32
-    ) + jnp.einsum("tf,df->td", d_upward, up_weight, preferred_element_type=jnp.float32)
+        "tf,fd->td", d_gate, gate_weight, preferred_element_type=jnp.float32
+    ) + jnp.einsum("tf,fd->td", d_upward, up_weight, preferred_element_type=jnp.float32)
     unused_two, norm_back_two = jax.vjp(norm_rows, middle, gain_two)
     d_middle_norm, grad_gain_two = norm_back_two(d_normed_two)
     d_middle = cotan + d_middle_norm
     d_branch = d_middle.astype(jnp.bfloat16)
-    grad_out = jnp.einsum("td,te->de", mixed, d_branch, preferred_element_type=jnp.float32)
-    d_mixed = jnp.einsum("te,de->td", d_branch, out_weight, preferred_element_type=jnp.float32)
+    grad_out = owned_sum(d_branch, mixed)
+    d_mixed = jnp.einsum("te,ed->td", d_branch, out_weight, preferred_element_type=jnp.float32)
     unused_three, conv_back = jax.vjp(mix_conv, projected, filters)
     d_projected, grad_filters = conv_back(d_mixed)
     d_projected = d_projected.astype(jnp.bfloat16)
-    grad_in = jnp.einsum("td,te->de", normed, d_projected, preferred_element_type=jnp.float32)
-    d_normed = jnp.einsum("te,de->td", d_projected, in_weight, preferred_element_type=jnp.float32)
+    grad_in = owned_sum(d_projected, normed)
+    d_normed = jnp.einsum("te,ed->td", d_projected, in_weight, preferred_element_type=jnp.float32)
     unused_four, norm_back_one = jax.vjp(norm_rows, resid, gain_one)
     d_resid_norm, grad_gain_one = norm_back_one(d_normed)
     input_grad = d_middle + d_resid_norm
-    grad_gains = jnp.stack([grad_gain_one, grad_gain_two])
-    owners = lax.axis_size(("dp", "fsdp"))
-    full_grads = (grad_in, grad_filters, grad_out, grad_gate, grad_up, grad_down, grad_gains)
-    packed = pack_owners(full_grads, owners)
-    own_row = lax.psum_scatter(packed, ("dp", "fsdp"), scatter_dimension=0, tiled=True)
-    owned = unpack_owned(own_row, full_grads, owners)
+    grad_small = jnp.concatenate([grad_filters, grad_gain_one[None], grad_gain_two[None]], axis=0)
+    grad_small = lax.psum(grad_small, shard_axes)
+    share = convtaps.shape[1]
+    grad_small = lax.dynamic_slice_in_dim(
+        grad_small, lax.axis_index(shard_axes) * share, share, axis=1
+    )
+    owned = (
+        grad_in,
+        grad_small[:KERNEL],
+        grad_out,
+        grad_gate,
+        grad_up,
+        grad_down,
+        grad_small[KERNEL:],
+    )
     outputs = [block_output, input_grad]
     for position in range(7):
         moment, square, updated = adamw_step(

time: 2120 us -> 1130 us (0.53)
  local copies, waits for them, and re-layouts: 551 us -> 24.2 us
  waiting for transfers between devices: 1290 us -> 835 us
    unnamed x7 -> x10, waiting for transfers between devices: 1030 us -> 0.16 us
    reduce_scatter x0 -> x5, waiting for transfers between devices: none -> 535 us  [owned_sum(): total = lax.psum_scatter(part, shard_axes, scatter_dimension=0, tiled=True)]
    reshape x10 -> x0, local copies, waits for them, and re-layouts: 254 us -> none  [pack_owners(): grad.reshape(rows, owners, share).transpose(1, 0, 2)]
    unnamed x115 -> x99, local copies, waits for them, and re-layouts: 204 us -> 24 us
    transpose x4 -> x0, local copies, waits for them, and re-layouts: 68.4 us -> none  [pack_owners(): grad.reshape(rows, owners, share).transpose(1, 0, 2)]
    psum x0 -> x1, blocking collectives: none -> 40 us  [shards(): grad_small = lax.psum(grad_small, shard_axes)]
    all_gather x5, waiting for transfers between devices: 262 us -> 299 us  [shards(): lax.all_gather(item.astype(jnp.bfloat16).T, shard_axes, axis=0, tiled=True)]
    all_gather x2 -> x1, blocking collectives: 79.9 us -> 43.7 us  [shards(): lax.all_gather(small, shard_axes, axis=1, tiled=True).astype(jnp.float32)]
  transfers between devices with their start and end apart: 6 -> 10, of which waited for: 5 -> 10; matrix products, arithmetic and copies ran while one was open for 3% -> 12% of each run, Pallas kernels for 0% -> 0%
where the time goes in v1:
time: 1130 us; the launch traced here: 1120 us
  waiting for transfers between devices  835 us (74%)
  matrix products  126 us (11%)
  blocking collectives  83.8 us (7%)
  other arithmetic  32.9 us (3%)
  local copies, waits for them, and re-layouts  24.2 us (2%)
  between operations  14.9 us (1%)
    reduce_scatter x5, waiting for transfers between devices, owned_sum(): total = lax.psum_scatter(part, shard_axes, scatter_dimension=0, tiled=True)  535 us
    all_gather x5, waiting for transfers between devices, shards(): lax.all_gather(item.astype(jnp.bfloat16).T, shard_axes, axis=0, tiled=True)  299 us
    all_gather x1, blocking collectives, shards(): lax.all_gather(small, shard_axes, axis=1, tiled=True).astype(jnp.float32)  43.7 us
    psum x1, blocking collectives, shards(): grad_small = lax.psum(grad_small, shard_axes)  40 us
    dot_general x5, matrix products, owned_sum(): jnp.einsum('te,td->ed', left, right, preferred_element_type=jnp.float32)  39.2 us
    unnamed x99, local copies, waits for them, and re-layouts  24 us
  transfers between devices with their start and end apart: 10, of which 10 were waited for; matrix products, arithmetic and copies ran while one was open for 12% of the time, Pallas kernels for 0%

profile of v1, /device:TPU:0, one launch (start us, length us, event | category | flops | bytes accessed | tf_op | source)
XLA Modules:
  0.0 1117.1 jit_solution(11643455606029356744)
XLA Ops:
  7.3 1.8 convert_bitcast_fusion.3
  9.1 1.6 convert_bitcast_fusion.4
  10.8 1.8 convert_bitcast_fusion.2
  14.5 43.7 %all-gather = bf16[32,32,5]{1,2,0:T(8,128)(2,1)S(1)} all-gather(bf16[1,32,5]{1,2,0:T(8,128)(2,1)S(1)} %maximum_bitcast_fusion), channel_id=1, replica_groups=mesh['dp'=8,'fsdp'=4] {'dp','fsdp'}, dimensions={0}, use_global_device_ids=true | all-gather | bytes 10560 | tf_op jit(solution)/shard_map/all_gather | solution.py:98
  58.6 25.3 %all-gather.7.cloned.1.call-done = bf16[3072,1024]{1,0:T(8,128)(2,1)} async-done(((bf16[96,1024]{1,0:T(8,128)(2,1)}), bf16[3072,1024]{1,0:T(8,128)(2,1)}) %all-gather.7.cloned.1.call-update) | async-done | bytes 6291472 | tf_op jit(solution)/shard_map/all_gather | solution.py:94
  83.9 5.8 fusion.29
  90.3 2.1 copy-done
  92.9 2.7 fusion.16
  95.7 46.6 %all-gather.9.cloned.1.call-done = bf16[1024,1024]{1,0:T(8,128)(2,1)} async-done(((bf16[32,1024]{1,0:T(8,128)(2,1)}), bf16[1024,1024]{1,0:T(8,128)(2,1)}) %all-gather.9.cloned.1.call-update) | async-done | bytes 2097168 | tf_op jit(solution)/shard_map/all_gather | solution.py:94
  142.3 3.3 multiply_reduce_fusion.3
  145.6 1.4 multiply_convert_fusion.2
  147.0 79.7 %all-gather.11.cloned.1.call-done = bf16[4608,1024]{1,0:T(8,128)(2,1)} async-done(((bf16[144,1024]{1,0:T(8,128)(2,1)}), bf16[4608,1024]{1,0:T(8,128)(2,1)}) %all-gather.11.cloned.1.call-update) | async-done | bytes 9437200 | tf_op jit(solution)/shard_map/all_gather | solution.py:94
  226.7 10.2 fusion.52
  236.9 73.9 %all-gather.13.cloned.1.call-done = bf16[4608,1024]{1,0:T(8,128)(2,1)} async-done(((bf16[144,1024]{1,0:T(8,128)(2,1)}), bf16[4608,1024]{1,0:T(8,128)(2,1)}) %all-gather.13.cloned.1.call-update) | async-done | bytes 9437200 | tf_op jit(solution)/shard_map/all_gather | solution.py:94
  310.7 10.2 fusion.53
  320.9 73.8 %all-gather.15.cloned.1.call-done = bf16[1024,4608]{1,0:T(8,128)(2,1)} async-done(((bf16[32,4608]{1,0:T(8,128)(2,1)}), bf16[1024,4608]{1,0:T(8,128)(2,1)}) %all-gather.15.cloned.1.call-update) | async-done | bytes 9437200 | tf_op jit(solution)/shard_map/all_gather | solution.py:94
  394.7 17.7 %multiply_convert_fusion = (bf16[512,4608]{1,0:T(8,128)(2,1)}, bf16[512,4608]{1,0:T(8,128)(2,1)}, bf16[512,4608]{1,0:T(8,128)(2,1)}) fusion(f32[512,4608]{1,0:T(8,128)} %fusion.52, f32[512,4608]{1,0:T(8,128)} %fusion.53, bf16[512,1024]{1,0:T(8,128)(2,1)} %param.24, bf16[1024,4608]{1,0:T(8,128)(2,1)} %all-gather.15.cloned.1.call-done), kind=kOutput, calls=%fused_computation.7 | convolution fusion | flops 4869586944 | bytes 43515904 | tf_op jit(solution)/shard_map/td,df->tf/dot_general | solution.py:122
  412.5 9.5 fusion.54
  422.0 5.4 multiply_reduce_fusion
  428.1 1.3 copy-done.4
  429.4 2.8 convolution_convert_fusion.4
  432.2 6.3 multiply_reduce_fusion.1
  438.5 1.0 multiply_bitcast_fusion.2
  440.3 1.3 slice_multiply_fusion.2
  441.6 1.3 copy-done.14
  443.5 6.5 convolution_convert_fusion.3
  450.1 1.1 copy-done.21
  451.3 10.1 convolution_convert_fusion.1
  461.4 9.9 convolution_convert_fusion.2
  471.5 1.1 copy-done.23
  472.6 9.9 fusion.4
  482.5 12.7 %copy.71 = bf16[1024,4608]{1,0:T(8,128)(2,1)} copy(bf16[1024,4608]{0,1:T(8,128)(2,1)} %fusion.4) | data formatting | bytes 18874368
  495.3 1.6 copy-done.2
  496.8 2.3 fusion.14
  499.7 8.7 fusion.8
  508.4 40.0 %psum.7 = f32[5,1024]{1,0:T(8,128)S(1)} all-reduce(f32[5,1024]{1,0:T(8,128)S(1)} %pad_maximum_fusion), channel_id=1, replica_groups=mesh['dp'=8,'fsdp'=4] {'dp','fsdp'}, use_global_device_ids=true, to_apply=%region_10.11 | all-reduce | flops 5120 | bytes 40960 | tf_op jit(solution)/shard_map/psum | solution.py:149
  549.8 3.6 fusion.10
  553.5 9.9 add_convert_fusion.1
  563.4 4.3 reduce-scatter.10.cloned.1.call-done
  567.7 1.6 multiply_subtract_fusion.4
  569.4 115.5 %reduce-scatter.8.cloned.1.call-done = bf16[96,1024]{1,0:T(8,128)(2,1)} async-done(((bf16[3072,1024]{1,0:T(8,128)(2,1)}), bf16[96,1024]{1,0:T(8,128)(2,1)}) %reduce-scatter.8.cloned.1.call-update) | async-done | bytes 196624 | tf_op jit(solution)/shard_map/reduce_scatter | solution.py:118
  684.9 2.1 multiply_subtract_fusion.3
  687.1 138.7 %reduce-scatter.14.cloned.1.call-done = bf16[144,1024]{1,0:T(8,128)(2,1)} async-done(((bf16[4608,1024]{1,0:T(8,128)(2,1)}), bf16[144,1024]{1,0:T(8,128)(2,1)}) %reduce-scatter.14.cloned.1.call-update) | async-done | bytes 294928 | tf_op jit(solution)/shard_map/reduce_scatter | solution.py:118
  825.8 2.5 multiply_subtract_fusion.1
  828.2 139.1 %reduce-scatter.12.cloned.1.call-done = bf16[144,1024]{1,0:T(8,128)(2,1)} async-done(((bf16[4608,1024]{1,0:T(8,128)(2,1)}), bf16[144,1024]{1,0:T(8,128)(2,1)}) %reduce-scatter.12.cloned.1.call-update) | async-done | bytes 294928 | tf_op jit(solution)/shard_map/reduce_scatter | solution.py:118
  967.3 2.5 multiply_subtract_fusion.2
  969.8 137.8 %reduce-scatter.16.cloned.1.call-done = bf16[32,4608]{1,0:T(8,128)(2,1)} async-done(((bf16[1024,4608]{1,0:T(8,128)(2,1)}), bf16[32,4608]{1,0:T(8,128)(2,1)}) %reduce-scatter.16.cloned.1.call-update) | async-done | bytes 294928 | tf_op jit(solution)/shard_map/reduce_scatter | solution.py:118
  1107.6 2.4 multiply_subtract_fusion
  (133 shorter events, 7.7 us)
Async XLA Ops:
  7.2 5.5 copy-start.9
  7.2 6.4 copy-start.12
  7.2 76.7 %all-gather.7.cloned.1.call-start = ((), (), s32[]{:S(2)}) async-start(), calls=%async_computation.5 | async-start | bytes 6488064 | tf_op jit(solution)/shard_map/all_gather | solution.py:94
  9.0 5.4 copy-start.37
  9.0 5.4 copy-start.41
  9.1 49.2 %copy-start.8 = (bf16[512,1024]{1,0:T(8,128)(2,1)S(1)}, bf16[512,1024]{1,0:T(8,128)(2,1)}, u32[]{:S(2)}) copy-start(bf16[512,1024]{1,0:T(8,128)(2,1)} %param.23) | copy-start | bytes 3145732
  9.1 133.2 %all-gather.9.cloned.1.call-start = ((), (), s32[]{:S(2)}) async-start(), calls=%async_computation.6 | async-start | bytes 2162688 | tf_op jit(solution)/shard_map/all_gather | solution.py:94
  10.8 215.9 %all-gather.11.cloned.1.call-start = ((), (), s32[]{:S(2)}) async-start(), calls=%async_computation.7 | async-start | bytes 9732096 | tf_op jit(solution)/shard_map/all_gather | solution.py:94
  12.7 298.0 %all-gather.13.cloned.1.call-start = ((), (), s32[]{:S(2)}) async-start(), calls=%async_computation.8 | async-start | bytes 9732096 | tf_op jit(solution)/shard_map/all_gather | solution.py:94
  13.5 381.2 %all-gather.15.cloned.1.call-start = ((), (), s32[]{:S(2)}) async-start(), calls=%async_computation.9 | async-start | bytes 9732096 | tf_op jit(solution)/shard_map/all_gather | solution.py:94
  14.3 553.4 %reduce-scatter.10.cloned.1.call-start = ((), (), s32[]{:S(2)}) async-start(), calls=%async_computation.11 | async-start | bytes 2162688 | tf_op jit(solution)/shard_map/reduce_scatter | solution.py:118
  58.6 31.1 %copy-start.35 = (f32[512]{0:T(512)}, f32[512]{0:T(512)S(1)}, u32[]{:S(2)}) copy-start(f32[512]{0:T(512)S(1)} %fusion.11) | copy-start | bytes 6148
  145.6 281.9 %copy-start.6 = (f32[512,1024]{1,0:T(8,128)}, f32[512,1024]{1,0:T(8,128)S(1)}, u32[]{:S(2)}) copy-start(f32[512,1024]{1,0:T(8,128)S(1)} %get-tuple-element.138) | copy-start | bytes 6291460
  412.4 9.5 copy-start.45
  412.5 9.5 copy-start.46
  422.0 5.5 copy-start.22
  429.4 10.9 slice-start
  432.2 252.7 %reduce-scatter.8.cloned.1.call-start = ((), (), s32[]{:S(2)}) async-start(), calls=%async_computation.10 | async-start | bytes 6488064 | tf_op jit(solution)/shard_map/reduce_scatter | solution.py:118
  432.2 8.0 slice-start.1
  438.5 3.0 copy-start.18
  450.1 375.7 %reduce-scatter.14.cloned.1.call-start = ((), (), s32[]{:S(2)}) async-start(), calls=%async_computation.13 | async-start | bytes 9732096 | tf_op jit(solution)/shard_map/reduce_scatter | solution.py:118
  461.4 505.9 %reduce-scatter.12.cloned.1.call-start = ((), (), s32[]{:S(2)}) async-start(), calls=%async_computation.12 | async-start | bytes 9732096 | tf_op jit(solution)/shard_map/reduce_scatter | solution.py:118
  471.4 636.1 %reduce-scatter.16.cloned.1.call-start = ((), (), s32[]{:S(2)}) async-start(), calls=%async_computation.14 | async-start | bytes 9732096 | tf_op jit(solution)/shard_map/reduce_scatter | solution.py:118
  496.8 2.9 copy-start.17
  499.7 48.9 %copy-start.36 = (f32[512]{0:T(512)S(1)}, f32[512]{0:T(512)}, u32[]{:S(2)}) copy-start(f32[512]{0:T(512)} %copy-done.35) | copy-start | bytes 6148
  499.7 48.9 %copy-start.42 = (f32[2,32]{1,0:T(2,128)S(1)}, f32[2,32]{1,0:T(2,128)}, u32[]{:S(2)}) copy-start(f32[2,32]{1,0:T(2,128)} %param.31) | copy-start | bytes 772
  499.7 48.9 %copy-start.43 = (f32[2,32]{1,0:T(2,128)S(1)}, f32[2,32]{1,0:T(2,128)}, u32[]{:S(2)}) copy-start(f32[2,32]{1,0:T(2,128)} %param.45) | copy-start | bytes 772
  499.7 48.9 %copy-start.44 = (f32[2,32]{1,0:T(2,128)S(1)}, f32[2,32]{1,0:T(2,128)}, u32[]{:S(2)}) copy-start(f32[2,32]{1,0:T(2,128)} %param.38) | copy-start | bytes 772
  499.7 49.5 %copy-start.38 = (f32[3,32]{1,0:T(4,128)S(1)}, f32[3,32]{1,0:T(4,128)}, u32[]{:S(2)}) copy-start(f32[3,32]{1,0:T(4,128)} %param.26) | copy-start | bytes 1156
  499.7 49.5 %copy-start.39 = (f32[3,32]{1,0:T(4,128)S(1)}, f32[3,32]{1,0:T(4,128)}, u32[]{:S(2)}) copy-start(f32[3,32]{1,0:T(4,128)} %param.40) | copy-start | bytes 1156
  499.7 49.5 %copy-start.40 = (f32[3,32]{1,0:T(4,128)S(1)}, f32[3,32]{1,0:T(4,128)}, u32[]{:S(2)}) copy-start(f32[3,32]{1,0:T(4,128)} %param.33) | copy-start | bytes 1156
  499.7 50.1 %copy-start.5 = (f32[512,1024]{1,0:T(8,128)S(1)}, f32[512,1024]{1,0:T(8,128)}, u32[]{:S(2)}) copy-start(f32[512,1024]{1,0:T(8,128)} %copy-done.4) | copy-start | bytes 6291460
  549.8 3.6 copy-start.7
  553.4 14.3 %copy-start.30 = (f32[1024,32]{0,1:T(8,128)S(1)}, f32[1024,32]{0,1:T(8,128)}, u32[]{:S(2)}) copy-start(f32[1024,32]{0,1:T(8,128)} %param.27) | copy-start | bytes 393220
  553.4 14.3 %copy-start.33 = (f32[1024,32]{0,1:T(8,128)S(1)}, f32[1024,32]{0,1:T(8,128)}, u32[]{:S(2)}) copy-start(f32[1024,32]{0,1:T(8,128)} %param.41) | copy-start | bytes 393220
  553.4 14.3 %copy-start.34 = (f32[1024,32]{0,1:T(8,128)S(1)}, f32[1024,32]{0,1:T(8,128)}, u32[]{:S(2)}) copy-start(f32[1024,32]{0,1:T(8,128)} %param.34) | copy-start | bytes 393220
  553.4 131.5 %copy-start.19 = (f32[1024,96]{0,1:T(8,128)S(1)}, f32[1024,96]{0,1:T(8,128)}, u32[]{:S(2)}) copy-start(f32[1024,96]{0,1:T(8,128)} %param.25) | copy-start | bytes 1179652
  553.4 131.5 %copy-start.31 = (f32[1024,96]{0,1:T(8,128)S(1)}, f32[1024,96]{0,1:T(8,128)}, u32[]{:S(2)}) copy-start(f32[1024,96]{0,1:T(8,128)} %param.39) | copy-start | bytes 1179652
  553.4 131.5 %copy-start.32 = (f32[1024,96]{0,1:T(8,128)S(1)}, f32[1024,96]{0,1:T(8,128)}, u32[]{:S(2)}) copy-start(f32[1024,96]{0,1:T(8,128)} %param.32) | copy-start | bytes 1179652
  563.4 262.4 %copy-start.10 = (f32[1024,144]{0,1:T(8,128)S(1)}, f32[1024,144]{0,1:T(8,128)}, u32[]{:S(2)}) copy-start(f32[1024,144]{0,1:T(8,128)} %param.29) | copy-start | bytes 1769476
  563.4 262.4 %copy-start.24 = (f32[1024,144]{0,1:T(8,128)S(1)}, f32[1024,144]{0,1:T(8,128)}, u32[]{:S(2)}) copy-start(f32[1024,144]{0,1:T(8,128)} %param.43) | copy-start | bytes 1769476
  563.4 262.4 %copy-start.25 = (f32[1024,144]{0,1:T(8,128)S(1)}, f32[1024,144]{0,1:T(8,128)}, u32[]{:S(2)}) copy-start(f32[1024,144]{0,1:T(8,128)} %param.36) | copy-start | bytes 1769476
  687.1 280.2 %copy-start.11 = (f32[1024,144]{0,1:T(8,128)S(1)}, f32[1024,144]{0,1:T(8,128)}, u32[]{:S(2)}) copy-start(f32[1024,144]{0,1:T(8,128)} %param.28) | copy-start | bytes 1769476
  687.1 280.2 %copy-start.26 = (f32[1024,144]{0,1:T(8,128)S(1)}, f32[1024,144]{0,1:T(8,128)}, u32[]{:S(2)}) copy-start(f32[1024,144]{0,1:T(8,128)} %param.42) | copy-start | bytes 1769476
  687.1 280.2 %copy-start.27 = (f32[1024,144]{0,1:T(8,128)S(1)}, f32[1024,144]{0,1:T(8,128)}, u32[]{:S(2)}) copy-start(f32[1024,144]{0,1:T(8,128)} %param.35) | copy-start | bytes 1769476
  828.2 279.3 %copy-start.13 = (f32[4608,32]{0,1:T(8,128)S(1)}, f32[4608,32]{0,1:T(8,128)}, u32[]{:S(2)}) copy-start(f32[4608,32]{0,1:T(8,128)} %param.30) | copy-start | bytes 1769476
  828.2 279.3 %copy-start.28 = (f32[4608,32]{0,1:T(8,128)S(1)}, f32[4608,32]{0,1:T(8,128)}, u32[]{:S(2)}) copy-start(f32[4608,32]{0,1:T(8,128)} %param.44) | copy-start | bytes 1769476
  828.2 279.3 %copy-start.29 = (f32[4608,32]{0,1:T(8,128)S(1)}, f32[4608,32]{0,1:T(8,128)}, u32[]{:S(2)}) copy-start(f32[4608,32]{0,1:T(8,128)} %param.37) | copy-start | bytes 1769476
  (11 other events, 20.0 us)
Sparse Core Ops, SparseCore 0:
  11.5 72.3 all-gather.6
  87.3 54.8 all-gather.8
  145.8 80.8 all-gather.10
  230.0 80.6 all-gather.12
  314.0 80.6 all-gather.14
  432.3 135.3 reduce-scatter.9
  574.3 110.5 reduce-scatter.7
  690.8 134.8 reduce-scatter.13
  832.7 134.5 reduce-scatter.11
  973.0 134.4 reduce-scatter.15

commit v2 on v1

--- a/solution.py
+++ b/solution.py
@@ -43,6 +43,117 @@
     vhat = square / (1.0 - beta_two**STEP)
     updated = param - rate * (mhat / (jnp.sqrt(vhat) + eps_adam) + decay * param)
     return (moment, square, updated)
+
+
+AXES = ("dp", "fsdp")
+CORES = 2
+
+
+def grid_shape():
+    rows = lax.axis_size("fsdp") // CORES
+    return {"z": lax.axis_size("dp") // rows, "x": rows, "y": rows, "c": CORES}
+
+
+def position(dim):
+    sizes = grid_shape()
+    index = lax.axis_index(AXES)
+    below = {"z": ("x", "y", "c"), "x": ("y", "c"), "y": ("c",), "c": ()}[dim]
+    for lower in below:
+        index = index // sizes[lower]
+    return index % sizes[dim]
+
+
+def shift_pairs(dim, step, allowed):
+    sizes = grid_shape()
+    stride = {
+        "z": sizes["x"] * sizes["y"] * sizes["c"],
+        "x": sizes["y"] * sizes["c"],
+        "y": sizes["c"],
+        "c": 1,
+    }[dim]
+    total = sizes["z"] * sizes["x"] * sizes["y"] * sizes["c"]
+    pairs = []
+    for device in range(total):
+        place = device // stride % sizes[dim]
+        if allowed(place) and 0 <= place + step < sizes[dim]:
+            pairs.append((device, device + step * stride))
+    return pairs
+
+
+def swap(value, dim):
+    pairs = shift_pairs(dim, 1, lambda place: True) + shift_pairs(dim, -1, lambda place: True)
+    return lax.ppermute(value, AXES, pairs)
+
+
+def line_gather(value, dim):
+    size = grid_shape()[dim]
+    place = position(dim)
+    if size == 2:
+        other = swap(value, dim)
+        first = place == 0
+        return jnp.stack([jnp.where(first, value, other), jnp.where(first, other, value)])
+    from_low = []
+    from_high = []
+    low = value
+    high = value
+    for step in range(1, size):
+        low = lax.ppermute(low, AXES, shift_pairs(dim, 1, lambda p: p >= step - 1))
+        high = lax.ppermute(high, AXES, shift_pairs(dim, -1, lambda p: p <= size - step))
+        from_low.append(low)
+        from_high.append(high)
+    every = jnp.stack(from_low[::-1] + [value] + from_high)
+    return lax.dynamic_slice_in_dim(every, size - 1 - place, size, axis=0)
+
+
+def mesh_gather(value, order):
+    shape = value.shape
+    for dim in order:
+        value = line_gather(value, dim)
+    names = order[::-1]
+    value = value.transpose([names.index(dim) for dim in "zxyc"] + [4, 5])
+    return value.reshape((-1,) + shape)
+
+
+def pick(parts, axis, index):
+    size = parts.shape[axis]
+    return lax.dynamic_index_in_dim(parts, jnp.clip(index, 0, size - 1), axis, keepdims=False)
+
+
+def add_low(left, right):
+    return (left.astype(jnp.float32) + right.astype(jnp.float32)).astype(jnp.bfloat16)
+
+
+def line_sum(parts, axis, dim, last):
+    size = grid_shape()[dim]
+    place = position(dim)
+    own = pick(parts, axis, place)
+    if size == 2:
+        arrived = swap(pick(parts, axis, 1 - place), dim).astype(jnp.float32)
+    else:
+        up = None
+        down = None
+        for step in range(1, size):
+            send_up = pick(parts, axis, place + size - step)
+            send_down = pick(parts, axis, place - size + step)
+            if step > 1:
+                send_up = add_low(send_up, up)
+                send_down = add_low(send_down, down)
+            up = lax.ppermute(send_up, AXES, shift_pairs(dim, 1, lambda p: p <= step - 1))
+            down = lax.ppermute(send_down, AXES, shift_pairs(dim, -1, lambda p: p >= size - step))
+        arrived = up.astype(jnp.float32) + down.astype(jnp.float32)
+    total = own.astype(jnp.float32) + arrived
+    return total if last else total.astype(jnp.bfloat16)
+
+
+def mesh_sum(parts, order):
+    sizes = grid_shape()
+    parts = parts.reshape(tuple(sizes[dim] for dim in "zxyc") + parts.shape[1:])
+    names = ["z", "x", "y", "c"]
+    for dim in order:
+        axis = names.index(dim)
+        names.pop(axis)
+        parts = line_sum(parts, axis, dim, len(names) == 0)
+    return parts
 
 
 def shards(
@@ -89,13 +200,24 @@
         second_downproj,
         second_normgains,
     )
-    shard_axes = ("dp", "fsdp")
-    in_weight, out_weight, gate_weight, up_weight, down_weight = (
-        lax.all_gather(item.astype(jnp.bfloat16).T, shard_axes, axis=0, tiled=True)
-        for item in (inproj, outproj, gateproj, upproj, downproj)
-    )
+    owners = lax.axis_size(AXES)
+    width = block_input.shape[1]
+    share = convtaps.shape[1]
+    low = [
+        item.astype(jnp.bfloat16).T for item in (inproj, outproj, gateproj, upproj, downproj)
+    ]
     small = jnp.concatenate([convtaps, normgains], axis=0).astype(jnp.bfloat16)
-    small = lax.all_gather(small, shard_axes, axis=1, tiled=True).astype(jnp.float32)
+    small = jnp.pad(small, ((0, 8 - KERNEL - 2), (0, width - share)))
+    rows_in, rows_out = low[0].shape[0], low[1].shape[0]
+    first = mesh_gather(jnp.concatenate([low[0], small]), "xyzc")
+    second = mesh_gather(jnp.concatenate([low[2], low[1]]), "yzxc")
+    up_weight = mesh_gather(low[3], "zxyc").reshape(-1, width)
+    down_weight = mesh_gather(low[4], "zxyc").reshape(width, -1)
+    in_weight = first[:, :rows_in].reshape(-1, width)
+    small = first[:, rows_in : rows_in + KERNEL + 2, :share]
+    small = small.transpose(1, 0, 2).reshape(KERNEL + 2, -1).astype(jnp.float32)
+    gate_weight = second[:, :-rows_out].reshape(-1, width)
+    out_weight = second[:, -rows_out:].reshape(-1, width)
     filters = small[:KERNEL]
     gain_one = small[KERNEL]
     gain_two = small[KERNEL + 1]
@@ -112,13 +234,12 @@
     block_output = (middle + ffn_out).astype(jnp.bfloat16)
     cotan = out_cotangent.astype(jnp.float32)
 
-    def owned_sum(left, right):
+    def gradient(left, right):
         part = jnp.einsum("te,td->ed", left, right, preferred_element_type=jnp.float32)
         part = part.astype(jnp.bfloat16)
-        total = lax.psum_scatter(part, shard_axes, scatter_dimension=0, tiled=True)
-        return total.astype(jnp.float32).T
-
-    grad_down = owned_sum(out_cotangent, hidden)
+        return part.reshape(owners, -1, part.shape[1])
+
+    grad_down = mesh_sum(gradient(out_cotangent, hidden), "cyxz").T
     d_hidden = jnp.einsum(
         "td,df->tf", out_cotangent, down_weight, preferred_element_type=jnp.float32
     )
@@ -126,8 +247,8 @@
     d_gate, d_upward = swiglu_back(d_hidden)
     d_gate = d_gate.astype(jnp.bfloat16)
     d_upward = d_upward.astype(jnp.bfloat16)
-    grad_gate = owned_sum(d_gate, normed_two)
-    grad_up = owned_sum(d_upward, normed_two)
+    grad_gate = mesh_sum(gradient(d_gate, normed_two), "cxzy").T
+    grad_up = mesh_sum(gradient(d_upward, normed_two), "cyxz").T
     d_normed_two = jnp.einsum(
         "tf,fd->td", d_gate, gate_weight, preferred_element_type=jnp.float32
     ) + jnp.einsum("tf,fd->td", d_upward, up_weight, preferred_element_type=jnp.float32)
@@ -135,22 +256,24 @@
     d_middle_norm, grad_gain_two = norm_back_two(d_normed_two)
     d_middle = cotan + d_middle_norm
     d_branch = d_middle.astype(jnp.bfloat16)
-    grad_out = owned_sum(d_branch, mixed)
+    grad_out = mesh_sum(gradient(d_branch, mixed), "cxzy").T
     d_mixed = jnp.einsum("te,ed->td", d_branch, out_weight, preferred_element_type=jnp.float32)
     unused_three, conv_back = jax.vjp(mix_conv, projected, filters)
     d_projected, grad_filters = conv_back(d_mixed)
     d_projected = d_projected.astype(jnp.bfloat16)
-    grad_in = owned_sum(d_projected, normed)
     d_normed = jnp.einsum("te,ed->td", d_projected, in_weight, preferred_element_type=jnp.float32)
     unused_four, norm_back_one = jax.vjp(norm_rows, resid, gain_one)
     d_resid_norm, grad_gain_one = norm_back_one(d_normed)
     input_grad = d_middle + d_resid_norm
     grad_small = jnp.concatenate([grad_filters, grad_gain_one[None], grad_gain_two[None]], axis=0)
-    grad_small = lax.psum(grad_small, shard_axes)
-    share = convtaps.shape[1]
-    grad_small = lax.dynamic_slice_in_dim(
-        grad_small, lax.axis_index(shard_axes) * share, share, axis=1
-    )
+    grad_small = grad_small.astype(jnp.bfloat16).reshape(KERNEL + 2, owners, share)
+    grad_small = jnp.pad(
+        grad_small.transpose(1, 0, 2), ((0, 0), (0, 8 - KERNEL - 2), (0, width - share))
+    )
+    grad_first = jnp.concatenate([gradient(d_projected, normed), grad_small], axis=1)
+    grad_first = mesh_sum(grad_first, "czyx")
+    grad_in = grad_first[:rows_in].T
+    grad_small = grad_first[rows_in : rows_in + KERNEL + 2, :share]
     owned = (
         grad_in,
         grad_small[:KERNEL],

time: 1130 us -> 750 us (0.66)
  waiting for transfers between devices: 835 us -> 261 us
  starting transfers between devices: 0.41 us -> 154 us
  other arithmetic: 32.9 us -> 125 us
  blocking collectives: 83.8 us -> 0 us
  local copies, waits for them, and re-layouts: 24.2 us -> 76.5 us
  between operations: 14.9 us -> 3.31 us
    reduce_scatter x5 -> x0, waiting for transfers between devices: 535 us -> none  [owned_sum(): total = lax.psum_scatter(part, shard_axes, scatter_dimension=0, tiled=True)]
    all_gather x5 -> x0, waiting for transfers between devices: 299 us -> none  [shards(): lax.all_gather(item.astype(jnp.bfloat16).T, shard_axes, axis=0, tiled=True)]
    ppermute x0 -> x81, waiting for transfers between devices: none -> 261 us  [the longest x27 137 us: swap(): return lax.ppermute(value, AXES, pairs)]
    ppermute x0 -> x81, starting transfers between devices: none -> 154 us  [the longest x15 73.9 us: line_sum(): lax.ppermute(send_up, AXES, shift_pairs(dim, 1, lambda p: p <= step - 1))]
    another operation x2 -> x27, other arithmetic: 0.01 us -> 64.5 us  [the longest x24 63.1 us: line_gather(): jnp.stack([jnp.where(first, value, other), jnp.where(first, other, value)])]
    all_gather x1 -> x0, blocking collectives: 43.7 us -> none  [shards(): lax.all_gather(small, shard_axes, axis=1, tiled=True).astype(jnp.float32)]
    psum x1 -> x0, blocking collectives: 40 us -> none  [shards(): grad_small = lax.psum(grad_small, shard_axes)]
    convert_element_type x1 -> x31, other arithmetic: 0.01 us -> 36.8 us  [the longest x15 29 us: line_sum(): return total if last else total.astype(jnp.bfloat16)]
  transfers between devices with their start and end apart: 10 -> 81, of which waited for: 10 -> 26; matrix products, arithmetic and copies ran while one was open for 12% -> 27% of each run, Pallas kernels for 0% -> 0%
where the time goes in v2:
time: 750 us; the launch traced here: 738 us
  waiting for transfers between devices  261 us (35%)
  starting transfers between devices  154 us (21%)
  other arithmetic  125 us (17%)
  matrix products  118 us (16%)
  local copies, waits for them, and re-layouts  76.5 us (10%)
    ppermute x27, waiting for transfers between devices, swap(): return lax.ppermute(value, AXES, pairs)  137 us
    ppermute x12, waiting for transfers between devices, line_gather(): lax.ppermute(high, AXES, shift_pairs(dim, -1, lambda p: p <= size - step))  76.4 us
    ppermute x15, starting transfers between devices, line_sum(): lax.ppermute(send_up, AXES, shift_pairs(dim, 1, lambda p: p <= step - 1))  73.9 us
    another operation x24, other arithmetic, line_gather(): jnp.stack([jnp.where(first, value, other), jnp.where(first, other, value)])  63.1 us
    dot_general x5, matrix products, gradient(): jnp.einsum('te,td->ed', left, right, preferred_element_type=jnp.float32)  37.4 us
    ppermute x15, waiting for transfers between devices, line_sum(): lax.ppermute(send_up, AXES, shift_pairs(dim, 1, lambda p: p <= step - 1))  33.8 us
    dynamic_slice x8, local copies, waits for them, and re-layouts, pick(): lax.dynamic_index_in_dim(parts, jnp.clip(index, 0, size - 1), axis, keepd...  29.5 us
    convert_element_type x15, other arithmetic, line_sum(): return total if last else total.astype(jnp.bfloat16)  29 us
  transfers between devices with their start and end apart: 81, of which 26 were waited for; matrix products, arithmetic and copies ran while one was open for 27% of the time, Pallas kernels for 0%

profile of v2, /device:TPU:0, one launch (start us, length us, event | category | flops | bytes accessed | tf_op | source)
XLA Modules:
  0.0 737.6 jit_solution(1175134939862672568)
XLA Ops:
  1.9 5.7 collective-permute-start.18
  9.9 5.3 collective-permute-start.27
  30.0 6.4 collective-permute-done.9
  38.0 5.1 collective-permute-start.10
  56.7 13.9 %collective-permute-done.23 = bf16[144,1024]{1,0:T(8,128)(2,1)S(1)} collective-permute-done((bf16[144,1024]{1,0:T(8,128)(2,1)S(1)}, bf16[144,1024]{1,0:T(8,128)(2,1)S(1)}, u32[]{:S(2)}, u32[]{:S(2)}) %collective-permute-start.23) | collective-permute-done | bytes 294944 | tf_op jit(solution)/shard_map/ppermute | solution.py:101
  78.3 20.3 %collective-permute-done.5 = bf16[2,2,104,1024]{3,2,0,1:T(8,128)(2,1)S(1)} collective-permute-done((bf16[2,2,104,1024]{3,2,0,1:T(8,128)(2,1)S(1)}, bf16[2,2,104,1024]{3,2,0,1:T(8,128)(2,1)S(1)}, u32[]{:S(2)}, u32[]{:S(2)}) %collective-permute-start.5) | collective-permute-done | bytes 852000 | tf_op jit(solution)/shard_map/ppermute | solution.py:101
  100.5 13.4 %collective-permute-done.14 = bf16[2,176,1024]{2,1,0:T(8,128)(2,1)S(1)} collective-permute-done((bf16[2,176,1024]{2,1,0:T(8,128)(2,1)S(1)}, bf16[2,176,1024]{2,1,0:T(8,128)(2,1)S(1)}, u32[]{:S(2)}, u32[]{:S(2)}) %collective-permute-start.14) | collective-permute-done | bytes 720928 | tf_op jit(solution)/shard_map/ppermute | solution.py:101
  126.8 5.5 collective-permute-done.6
  134.9 12.8 %collective-permute-done.15 = bf16[2,176,1024]{2,1,0:T(8,128)(2,1)S(1)} collective-permute-done((bf16[2,176,1024]{2,1,0:T(8,128)(2,1)S(1)}, bf16[2,176,1024]{2,1,0:T(8,128)(2,1)S(1)}, u32[]{:S(2)}, u32[]{:S(2)}) %collective-permute-start.15) | collective-permute-done | bytes 720928 | tf_op jit(solution)/shard_map/ppermute | solution.py:101
  152.8 8.8 %collective-permute-done.7 = bf16[2,2,104,1024]{3,2,0,1:T(8,128)(2,1)S(1)} collective-permute-done((bf16[2,2,104,1024]{3,2,0,1:T(8,128)(2,1)S(1)}, bf16[2,2,104,1024]{3,2,0,1:T(8,128)(2,1)S(1)}, u32[]{:S(2)}, u32[]{:S(2)}) %collective-permute-start.7) | collective-permute-done | bytes 852000 | tf_op jit(solution)/shard_map/ppermute | solution.py:101
  165.3 12.2 %collective-permute-done.25 = bf16[2,4,144,1024]{3,2,0,1:T(8,128)(2,1)} collective-permute-done((bf16[2,4,144,1024]{3,2,0,1:T(8,128)(2,1)}, bf16[2,4,144,1024]{3,2,0,1:T(8,128)(2,1)}, u32[]{:S(2)}, u32[]{:S(2)}) %collective-permute-start.25) | collective-permute-done | bytes 2359328 | tf_op jit(solution)/shard_map/ppermute | solution.py:85
  183.4 38.8 %collective-permute-done.34 = bf16[2,4,32,4608]{3,2,0,1:T(8,128)(2,1)} collective-permute-done((bf16[2,4,32,4608]{3,2,0,1:T(8,128)(2,1)}, bf16[2,4,32,4608]{3,2,0,1:T(8,128)(2,1)}, u32[]{:S(2)}, u32[]{:S(2)}) %collective-permute-start.34) | collective-permute-done | bytes 2359328 | tf_op jit(solution)/shard_map/ppermute | solution.py:85
  245.1 6.5 fusion.60
  258.5 6.2 select_bitcast_fusion.5
  264.7 8.2 %pad_maximum_fusion.1 = bf16[2,2,2,4,144,1024]{5,4,0,1,2,3:T(8,128)(2,1)} fusion(bf16[1,2,2,4,144,1024]{5,4,0,1,2,3:T(8,128)(2,1)} %get-tuple-element.75, bf16[1,2,2,4,144,1024]{5,4,0,1,2,3:T(8,128)(2,1)} %get-tuple-element.74), kind=kLoop, calls=%fused_computation.8 | loop fusion | flops 4718592 | bytes 18874368 | tf_op jit(solution)/shard_map/stack | solution.py:94
  272.9 8.3 %select_bitcast_fusion.3 = (bf16[1,2,2,4,32,4608]{5,4,0,1,2,3:T(8,128)(2,1)}, bf16[1,2,2,4,32,4608]{5,4,0,1,2,3:T(8,128)(2,1)}) fusion(bf16[2,2,4,32,4608]{4,3,0,1,2:T(8,128)(2,1)} %collective-permute-done.35, pred[]{:T(512)S(6)} %eq.55, bf16[1,2,4,32,4608]{4,3,0,1,2:T(8,128)(2,1)} %copy-done.8, bf16[1,2,4,32,4608]{4,3,0,1,2:T(8,128)(2,1)} %copy-done.7), kind=kLoop, calls=%fused_computation.49 | loop fusion | flops 7077888 | bytes 18874368 | tf_op jit(solution)/shard_map/stack | solution.py:94
  281.2 8.3 %pad_maximum_fusion.2 = bf16[2,2,2,4,32,4608]{5,4,0,1,2,3:T(8,128)(2,1)} fusion(bf16[1,2,2,4,32,4608]{5,4,0,1,2,3:T(8,128)(2,1)} %get-tuple-element.73, bf16[1,2,2,4,32,4608]{5,4,0,1,2,3:T(8,128)(2,1)} %get-tuple-element.72), kind=kLoop, calls=%fused_computation.9 | loop fusion | flops 4718592 | bytes 18874368 | tf_op jit(solution)/shard_map/stack | solution.py:94
  299.9 9.2 %slice.102 = bf16[32,144,1024]{2,1,0:T(8,128)(2,1)} slice(bf16[32,176,1024]{2,1,0:T(8,128)(2,1)} %bitcast.464), slice={[0:32], [0:144], [0:1024]} | slice | bytes 18874368 | tf_op jit(solution)/shard_map/slice | solution.py:219
  313.6 7.4 %fusion.88 = f32[512,4608]{1,0:T(8,128)} fusion(bf16[512,1024]{1,0:T(8,128)(2,1)S(1)} %multiply_convert_fusion.1, bf16[4608,1024]{1,0:T(8,128)(2,1)S(1)} %bitcast.485), kind=kOutput, calls=%fused_computation.313 | convolution fusion | flops 4831838208 | bytes 19922944 | tf_op jit(solution)/shard_map/td,fd->tf/dot_general | solution.py:230
  321.0 7.7 %fusion.89 = f32[512,4608]{1,0:T(8,128)} fusion(bf16[512,1024]{1,0:T(8,128)(2,1)S(1)} %multiply_convert_fusion.1, bf16[4608,1024]{1,0:T(8,128)(2,1)S(1)} %bitcast.481), kind=kOutput, calls=%fused_computation.314 | convolution fusion | flops 4831838208 | bytes 19922944 | tf_op jit(solution)/shard_map/td,fd->tf/dot_general | solution.py:231
  328.7 17.9 %fusion.6 = (bf16[512,4608]{1,0:T(8,128)(2,1)}, bf16[512,4608]{1,0:T(8,128)(2,1)}, bf16[512,4608]{1,0:T(8,128)(2,1)}) fusion(f32[512,4608]{1,0:T(8,128)} %fusion.88, f32[512,4608]{1,0:T(8,128)} %fusion.89, bf16[512,1024]{1,0:T(8,128)(2,1)} %param.24, bf16[1024,4608]{1,0:T(8,128)(2,1)} %bitcast.475), kind=kOutput, calls=%fused_computation.18 | convolution fusion | flops 4869586944 | bytes 43515904 | tf_op jit(solution)/shard_map/td,df->tf/dot_general | solution.py:243
  346.6 9.1 %fusion.90 = f32[512,1024]{1,0:T(8,128)S(1)} fusion(bf16[512,4608]{1,0:T(8,128)(2,1)} %get-tuple-element.60, bf16[4608,1024]{1,0:T(8,128)(2,1)} %bitcast.484), kind=kOutput, calls=%fused_computation.315 | convolution fusion | flops 4831838208 | bytes 16252928 | tf_op jit(solution)/shard_map/tf,fd->td/dot_general | solution.py:252
  355.8 8.3 %multiply_reduce_fusion = (bf16[1024]{0:T(1024)(128)(2,1)S(1)}, f32[512]{0:T(512)S(1)}, f32[512,1024]{1,0:T(8,128)S(1)}) fusion(f32[512,1024]{1,0:T(8,128)S(1)} %get-tuple-element.123, f32[512]{0:T(512)S(1)} %fusion.77, f32[1024]{0:T(1024)S(1)} %mul.553, f32[512,1024]{1,0:T(8,128)S(1)} %fusion.90, bf16[512,4608]{1,0:T(8,128)(2,1)S(1)} %copy-done.60, ...), kind=kOutput, calls=%fused_computation.101 | convolution fusion | flops 4835506688 | bytes 20457472 | tf_op jit(solution)/shard_map/tf,fd->td/dot_general | solution.py:254
  372.5 8.3 %fusion.19 = (bf16[1024]{0:T(1024)(128)(2,1)S(1)}, f32[512]{0:T(512)S(1)}, f32[512,1024]{1,0:T(8,128)}) fusion(bf16[512,1024]{1,0:T(8,128)(2,1)S(1)} %copy-done.25, f32[512]{0:T(512)S(1)} %fusion.76, f32[1024]{0:T(1024)S(1)} %mul.535, bf16[3072,1024]{1,0:T(8,128)(2,1)S(1)} %bitcast.493, f32[512,1024]{1,0:T(8,128)} %get-tuple-element.63, ...), kind=kOutput, calls=%fused_computation.83 | convolution fusion | flops 3229612544 | bytes 15738880 | tf_op jit(solution)/shard_map/te,ed->td/dot_general | solution.py:264
  380.8 8.0 %convolution_convert_fusion.3 = bf16[3072,1024]{1,0:T(8,128)(2,1)} fusion(bf16[512,1024]{1,0:T(8,128)(2,1)S(1)} %copy-done.25, f32[1024]{0:T(1024)S(1)} %mul.535, f32[512]{0:T(512)S(1)} %fusion.76, f32[512,1024]{1,0:T(8,128)S(1)} %copy-done.31, f32[512,1024]{1,0:T(8,128)S(1)} %copy-done.30, f32[512,1024]{1,0:T(8,128)} %get-tuple-element.100), kind=kOutput, calls=%fused_computation.33 | convolution fusion | flops 3231186944 | bytes 13637632 | tf_op jit(solution)/shard_map/te,td->ed/dot_general | solution.py:238
  392.0 7.9 %convolution_convert_fusion.2 = bf16[4608,1024]{1,0:T(8,128)(2,1)} fusion(bf16[512,4608]{1,0:T(8,128)(2,1)S(1)} %bitcast.504, bf16[512,1024]{1,0:T(8,128)(2,1)S(1)} %copy-done.36), kind=kOutput, calls=%fused_computation.4 | convolution fusion | flops 4836556800 | bytes 15204352 | tf_op jit(solution)/shard_map/te,td->ed/dot_general | solution.py:238
  400.6 10.2 %convolution_convert_fusion.1 = bf16[4608,1024]{1,0:T(8,128)(2,1)} fusion(bf16[512,4608]{1,0:T(8,128)(2,1)} %get-tuple-element.59, bf16[512,1024]{1,0:T(8,128)(2,1)S(1)} %copy-done.36), kind=kOutput, calls=%fused_computation.3 | convolution fusion | flops 4836556800 | bytes 15204352 | tf_op jit(solution)/shard_map/te,td->ed/dot_general | solution.py:238
  416.6 7.4 %constant_dynamic-slice_fusion.5 = (bf16[4,2,2,1,144,1024]{5,4,3,2,1,0:T(8,128)(2,1)}, bf16[4,2,2,1,144,1024]{5,4,3,2,1,0:T(8,128)(2,1)S(1)}) fusion(bf16[4,2,2,2,144,1024]{5,4,3,2,1,0:T(8,128)(2,1)} %bitcast.477, s32[]{:T(128)S(6)} %min.92, s32[]{:T(128)S(6)} %min.93), kind=kLoop, calls=%fused_computation.283 | loop fusion | bytes 18874376 | tf_op jit(solution)/shard_map/jit(dynamic_index_in_dim)/dynamic_slice | solution.py:119
  429.0 7.7 %collective-permute-start.47 = (bf16[2,32,1024]{2,1,0:T(8,128)(2,1)}, bf16[2,32,1024]{2,1,0:T(8,128)(2,1)S(1)}, u32[]{:S(2)}, u32[]{:S(2)}) collective-permute-start(bf16[2,32,1024]{2,1,0:T(8,128)(2,1)} %get-tuple-element.118), channel_id=1, source_target_pairs={{0,8},{1,9},{2,10},{3,11},{4,12},{5,13},{6,14},{7,15}} | collective-permute-start | bytes 393224 | tf_op jit(solution)/shard_map/ppermute | solution.py:141
  436.7 7.3 constant_dynamic-slice_fusion.3
  449.0 10.0 %convolution_convert_fusion = bf16[4608,1024]{0,1:T(8,128)(2,1)} fusion(bf16[512,4608]{1,0:T(8,128)(2,1)} %get-tuple-element.61, bf16[512,1024]{1,0:T(8,128)(2,1)S(1)} %copy-done.38), kind=kOutput, calls=%fused_computation.2 | convolution fusion | flops 4836556800 | bytes 15204352 | tf_op jit(solution)/shard_map/te,td->ed/dot_general | solution.py:238
  460.5 6.8 constant_dynamic-slice_fusion.1
  480.8 5.5 collective-permute-start.37
  486.3 9.9 %add_convert_fusion.1 = bf16[512,1024]{1,0:T(8,128)(2,1)} fusion(f32[512,1024]{1,0:T(8,128)S(1)} %copy-done.17, bf16[512,4608]{1,0:T(8,128)(2,1)} %get-tuple-element.61, bf16[1024,4608]{1,0:T(8,128)(2,1)} %bitcast.476), kind=kOutput, calls=%fused_computation.107 | convolution fusion | flops 4832886784 | bytes 17301504 | tf_op jit(solution)/shard_map/tf,df->td/dot_general | solution.py:233
  499.3 5.5 collective-permute-done.37
  506.8 5.5 collective-permute-start.38
  532.7 5.2 fusion.3
  539.8 18.0 %collective-permute-start.39 = (bf16[2,2,104,1024]{3,2,0,1:T(8,128)(2,1)S(1)}, bf16[2,2,104,1024]{3,2,0,1:T(8,128)(2,1)S(1)}, u32[]{:S(2)}, u32[]{:S(2)}) collective-permute-start(bf16[2,2,104,1024]{3,2,0,1:T(8,128)(2,1)S(1)} %get-tuple-element.86), channel_id=1, source_target_pairs={{0,8},{1,9},{2,10},{3,11},{4,12},{5,13},{6,14},{7,15},{8,16},{9,17... | collective-permute-start | bytes 2555912 | tf_op jit(solution)/shard_map/ppermute | solution.py:141
  563.1 10.7 %collective-permute-done.39 = bf16[2,2,104,1024]{3,2,0,1:T(8,128)(2,1)S(1)} collective-permute-done((bf16[2,2,104,1024]{3,2,0,1:T(8,128)(2,1)S(1)}, bf16[2,2,104,1024]{3,2,0,1:T(8,128)(2,1)S(1)}, u32[]{:S(2)}, u32[]{:S(2)}) %collective-permute-start.39) | collective-permute-done | bytes 852000 | tf_op jit(solution)/shard_map/ppermute | solution.py:141
  591.1 40.1 %collective-permute-done.73 = bf16[4,2,32,4608]{3,2,0,1:T(8,128)(2,1)S(1)} collective-permute-done((bf16[4,2,32,4608]{3,2,0,1:T(8,128)(2,1)S(1)}, bf16[4,2,32,4608]{3,2,0,1:T(8,128)(2,1)S(1)}, u32[]{:S(2)}, u32[]{:S(2)}) %collective-permute-start.73) | collective-permute-done | bytes 2359328 | tf_op jit(solution)/shard_map/ppermute | solution.py:85
  632.0 6.1 collective-permute-done.43
  640.6 6.0 collective-permute-done.44
  651.0 17.8 %collective-permute-done.74 = bf16[4,32,4608]{2,1,0:T(8,128)(2,1)S(1)} collective-permute-done((bf16[4,32,4608]{2,1,0:T(8,128)(2,1)S(1)}, bf16[4,32,4608]{2,1,0:T(8,128)(2,1)S(1)}, u32[]{:S(2)}, u32[]{:S(2)}) %collective-permute-start.74) | collective-permute-done | bytes 1179680 | tf_op jit(solution)/shard_map/ppermute | solution.py:85
  684.6 6.2 collective-permute-done.57
  692.0 5.0 collective-permute-start.58
  698.0 5.4 collective-permute-done.76
  705.8 8.3 %collective-permute-start.68 = (bf16[144,1024]{1,0:T(8,128)(2,1)S(1)}, bf16[144,1024]{1,0:T(8,128)(2,1)S(1)}, u32[]{:S(2)}, u32[]{:S(2)}) collective-permute-start(bf16[144,1024]{1,0:T(8,128)(2,1)S(1)} %get-tuple-element.108), channel_id=1, source_target_pairs={{0,8},{1,9},{2,10},{3,11},{4,12},{5,13},{6,14},{7,15},{8,16},{9,17... | collective-permute-start | bytes 884744 | tf_op jit(solution)/shard_map/ppermute | solution.py:141
  727.2 5.3 collective-permute-done.80
  (457 shorter events, 255.1 us)
Async XLA Ops:
  1.9 24.9 %collective-permute-start.18 = (bf16[144,1024]{1,0:T(8,128)(2,1)S(1)}, bf16[144,1024]{1,0:T(8,128)(2,1)}, u32[]{:S(2)}, u32[]{:S(2)}) collective-permute-start(bf16[144,1024]{1,0:T(8,128)(2,1)S(1)} %convert_bitcast_fusion.3), channel_id=1, source_target_pairs={{0,8},{1,9},{2,10},{3,11},{4,12},{5,13},{6,14},{7,15},{8,16},{9,17... | collective-permute-start | bytes 884744 | tf_op jit(solution)/shard_map/ppermute | solution.py:100
  38.0 37.2 %collective-permute-start.10 = (bf16[2,176,1024]{2,1,0:T(8,128)(2,1)S(1)}, bf16[2,176,1024]{2,1,0:T(8,128)(2,1)S(1)}, u32[]{:S(2)}, u32[]{:S(2)}) collective-permute-start(bf16[2,176,1024]{2,1,0:T(8,128)(2,1)S(1)} %pad_maximum_fusion.10), channel_id=1, source_target_pairs={{0,8},{1,9},{2,10},{3,11},{4,12},{5,13},{6,14},{7,15},{8,16},{9,17... | collective-permute-start | bytes 2162696 | tf_op jit(solution)/shard_map/ppermute | solution.py:100
  44.0 32.0 %collective-permute-start.13 = (bf16[2,176,1024]{2,1,0:T(8,128)(2,1)S(1)}, bf16[2,176,1024]{2,1,0:T(8,128)(2,1)S(1)}, u32[]{:S(2)}, u32[]{:S(2)}) collective-permute-start(bf16[2,176,1024]{2,1,0:T(8,128)(2,1)S(1)} %pad_maximum_fusion.10), channel_id=1, source_target_pairs={{8,0},{9,1},{10,2},{11,3},{12,4},{13,5},{14,6},{15,7},{16,8},{17,9... | collective-permute-start | bytes 2162696 | tf_op jit(solution)/shard_map/ppermute | solution.py:101
  45.4 25.1 %collective-permute-start.23 = (bf16[144,1024]{1,0:T(8,128)(2,1)S(1)}, bf16[144,1024]{1,0:T(8,128)(2,1)S(1)}, u32[]{:S(2)}, u32[]{:S(2)}) collective-permute-start(bf16[144,1024]{1,0:T(8,128)(2,1)S(1)} %collective-permute-done.22), channel_id=1, source_target_pairs={{8,0},{9,1},{10,2},{11,3},{12,4},{13,5},{14,6},{15,7}} | collective-permute-start | bytes 884744 | tf_op jit(solution)/shard_map/ppermute | solution.py:101
  47.4 26.3 %collective-permute-start.32 = (bf16[32,4608]{1,0:T(8,128)(2,1)S(1)}, bf16[32,4608]{1,0:T(8,128)(2,1)S(1)}, u32[]{:S(2)}, u32[]{:S(2)}) collective-permute-start(bf16[32,4608]{1,0:T(8,128)(2,1)S(1)} %collective-permute-done.31), channel_id=1, source_target_pairs={{8,0},{9,1},{10,2},{11,3},{12,4},{13,5},{14,6},{15,7}} | collective-permute-start | bytes 884744 | tf_op jit(solution)/shard_map/ppermute | solution.py:101
  49.8 27.5 %collective-permute-start.2 = (bf16[2,2,104,1024]{3,2,0,1:T(8,128)(2,1)S(1)}, bf16[2,2,104,1024]{3,2,0,1:T(8,128)(2,1)S(1)}, u32[]{:S(2)}, u32[]{:S(2)}) collective-permute-start(bf16[2,2,104,1024]{3,2,0,1:T(8,128)(2,1)S(1)} %pad_maximum_fusion.9), channel_id=1, source_target_pairs={{0,8},{1,9},{2,10},{3,11},{4,12},{5,13},{6,14},{7,15},{8,16},{9,17... | collective-permute-start | bytes 2555912 | tf_op jit(solution)/shard_map/ppermute | solution.py:100
  70.6 28.0 %collective-permute-start.5 = (bf16[2,2,104,1024]{3,2,0,1:T(8,128)(2,1)S(1)}, bf16[2,2,104,1024]{3,2,0,1:T(8,128)(2,1)S(1)}, u32[]{:S(2)}, u32[]{:S(2)}) collective-permute-start(bf16[2,2,104,1024]{3,2,0,1:T(8,128)(2,1)S(1)} %pad_maximum_fusion.9), channel_id=1, source_target_pairs={{8,0},{9,1},{10,2},{11,3},{12,4},{13,5},{14,6},{15,7},{16,8},{17,9... | collective-permute-start | bytes 2555912 | tf_op jit(solution)/shard_map/ppermute | solution.py:101
  73.7 41.0 %collective-permute-start.24 = (bf16[4,144,1024]{2,1,0:T(8,128)(2,1)S(1)}, bf16[4,144,1024]{2,1,0:T(8,128)(2,1)S(1)}, u32[]{:S(2)}, u32[]{:S(2)}) collective-permute-start(bf16[4,144,1024]{2,1,0:T(8,128)(2,1)S(1)} %constant_dynamic-slice_fusion.9), channel_id=1, source_target_pairs={{0,4},{1,5},{2,6},{3,7},{8,12},{9,13},{10,14},{11,15},{16,20},{17,... | collective-permute-start | bytes 3538952 | tf_op jit(solution)/shard_map/ppermute | solution.py:85
  75.2 24.0 %collective-permute-start.11 = (bf16[2,176,1024]{2,1,0:T(8,128)(2,1)S(1)}, bf16[2,176,1024]{2,1,0:T(8,128)(2,1)S(1)}, u32[]{:S(2)}, u32[]{:S(2)}) collective-permute-start(bf16[2,176,1024]{2,1,0:T(8,128)(2,1)S(1)} %collective-permute-done.10), channel_id=1, source_target_pairs={{8,16},{9,17},{10,18},{11,19},{12,20},{13,21},{14,22},{15,23},{16,... | collective-permute-start | bytes 2162696 | tf_op jit(solution)/shard_map/ppermute | solution.py:100
  76.0 38.0 %collective-permute-start.14 = (bf16[2,176,1024]{2,1,0:T(8,128)(2,1)S(1)}, bf16[2,176,1024]{2,1,0:T(8,128)(2,1)S(1)}, u32[]{:S(2)}, u32[]{:S(2)}) collective-permute-start(bf16[2,176,1024]{2,1,0:T(8,128)(2,1)S(1)} %collective-permute-done.13), channel_id=1, source_target_pairs={{8,0},{9,1},{10,2},{11,3},{12,4},{13,5},{14,6},{15,7},{16,8},{17,9... | collective-permute-start | bytes 2162696 | tf_op jit(solution)/shard_map/ppermute | solution.py:101
  77.4 45.6 %collective-permute-start.33 = (bf16[4,32,4608]{2,1,0:T(8,128)(2,1)S(1)}, bf16[4,32,4608]{2,1,0:T(8,128)(2,1)S(1)}, u32[]{:S(2)}, u32[]{:S(2)}) collective-permute-start(bf16[4,32,4608]{2,1,0:T(8,128)(2,1)S(1)} %constant_dynamic-slice_fusion.8), channel_id=1, source_target_pairs={{0,4},{1,5},{2,6},{3,7},{8,12},{9,13},{10,14},{11,15},{16,20},{17,... | collective-permute-start | bytes 3538952 | tf_op jit(solution)/shard_map/ppermute | solution.py:85
  98.5 27.7 %collective-permute-start.3 = (bf16[2,2,104,1024]{3,2,0,1:T(8,128)(2,1)S(1)}, bf16[2,2,104,1024]{3,2,0,1:T(8,128)(2,1)S(1)}, u32[]{:S(2)}, u32[]{:S(2)}) collective-permute-start(bf16[2,2,104,1024]{3,2,0,1:T(8,128)(2,1)S(1)} %collective-permute-done.2), channel_id=1, source_target_pairs={{8,16},{9,17},{10,18},{11,19},{12,20},{13,21},{14,22},{15,23},{16,... | collective-permute-start | bytes 2555912 | tf_op jit(solution)/shard_map/ppermute | solution.py:100
  99.2 33.0 %collective-permute-start.6 = (bf16[2,2,104,1024]{3,2,0,1:T(8,128)(2,1)S(1)}, bf16[2,2,104,1024]{3,2,0,1:T(8,128)(2,1)S(1)}, u32[]{:S(2)}, u32[]{:S(2)}) collective-permute-start(bf16[2,2,104,1024]{3,2,0,1:T(8,128)(2,1)S(1)} %collective-permute-done.5), channel_id=1, source_target_pairs={{8,0},{9,1},{10,2},{11,3},{12,4},{13,5},{14,6},{15,7},{16,8},{17,9... | collective-permute-start | bytes 2555912 | tf_op jit(solution)/shard_map/ppermute | solution.py:101
  114.7 33.0 %collective-permute-start.15 = (bf16[2,176,1024]{2,1,0:T(8,128)(2,1)S(1)}, bf16[2,176,1024]{2,1,0:T(8,128)(2,1)S(1)}, u32[]{:S(2)}, u32[]{:S(2)}) collective-permute-start(bf16[2,176,1024]{2,1,0:T(8,128)(2,1)S(1)} %collective-permute-done.14), channel_id=1, source_target_pairs={{8,0},{9,1},{10,2},{11,3},{12,4},{13,5},{14,6},{15,7}} | collective-permute-start | bytes 2162696 | tf_op jit(solution)/shard_map/ppermute | solution.py:101
  123.0 54.5 %collective-permute-start.25 = (bf16[2,4,144,1024]{3,2,0,1:T(8,128)(2,1)}, bf16[2,4,144,1024]{3,2,0,1:T(8,128)(2,1)}, u32[]{:S(2)}, u32[]{:S(2)}) collective-permute-start(bf16[2,4,144,1024]{3,2,0,1:T(8,128)(2,1)} %pad_maximum_fusion.7), channel_id=1, source_target_pairs={{0,2},{1,3},{4,6},{5,7},{8,10},{9,11},{12,14},{13,15},{16,18},{17,... | collective-permute-start | bytes 7077896 | tf_op jit(solution)/shard_map/ppermute | solution.py:85
  126.2 95.9 %collective-permute-start.34 = (bf16[2,4,32,4608]{3,2,0,1:T(8,128)(2,1)}, bf16[2,4,32,4608]{3,2,0,1:T(8,128)(2,1)}, u32[]{:S(2)}, u32[]{:S(2)}) collective-permute-start(bf16[2,4,32,4608]{3,2,0,1:T(8,128)(2,1)} %pad_maximum_fusion.8), channel_id=1, source_target_pairs={{0,2},{1,3},{4,6},{5,7},{8,10},{9,11},{12,14},{13,15},{16,18},{17,... | collective-permute-start | bytes 7077896 | tf_op jit(solution)/shard_map/ppermute | solution.py:85
  132.2 20.2 %collective-permute-start.4 = (bf16[2,2,104,1024]{3,2,0,1:T(8,128)(2,1)S(1)}, bf16[2,2,104,1024]{3,2,0,1:T(8,128)(2,1)S(1)}, u32[]{:S(2)}, u32[]{:S(2)}) collective-permute-start(bf16[2,2,104,1024]{3,2,0,1:T(8,128)(2,1)S(1)} %collective-permute-done.3), channel_id=1, source_target_pairs={{16,24},{17,25},{18,26},{19,27},{20,28},{21,29},{22,30},{23,31}} | collective-permute-start | bytes 2555912 | tf_op jit(solution)/shard_map/ppermute | solution.py:100
  133.0 28.6 %collective-permute-start.7 = (bf16[2,2,104,1024]{3,2,0,1:T(8,128)(2,1)S(1)}, bf16[2,2,104,1024]{3,2,0,1:T(8,128)(2,1)S(1)}, u32[]{:S(2)}, u32[]{:S(2)}) collective-permute-start(bf16[2,2,104,1024]{3,2,0,1:T(8,128)(2,1)S(1)} %collective-permute-done.6), channel_id=1, source_target_pairs={{8,0},{9,1},{10,2},{11,3},{12,4},{13,5},{14,6},{15,7}} | collective-permute-start | bytes 2555912 | tf_op jit(solution)/shard_map/ppermute | solution.py:101
  150.9 77.0 %collective-permute-start.16 = (bf16[4,2,176,1024]{3,2,1,0:T(8,128)(2,1)}, bf16[4,2,176,1024]{3,2,1,0:T(8,128)(2,1)}, u32[]{:S(2)}, u32[]{:S(2)}) collective-permute-start(bf16[4,2,176,1024]{3,2,1,0:T(8,128)(2,1)} %constant_dynamic-slice_fusion.10), channel_id=1, source_target_pairs={{0,4},{1,5},{2,6},{3,7},{8,12},{9,13},{10,14},{11,15},{16,20},{17,... | collective-permute-start | bytes 8650760 | tf_op jit(solution)/shard_map/ppermute | solution.py:85
  165.2 69.1 %collective-permute-start.8 = (bf16[4,2,2,104,1024]{4,3,1,2,0:T(8,128)(2,1)}, bf16[4,2,2,104,1024]{4,3,1,2,0:T(8,128)(2,1)}, u32[]{:S(2)}, u32[]{:S(2)}) collective-permute-start(bf16[4,2,2,104,1024]{4,3,1,2,0:T(8,128)(2,1)} %constant_dynamic-slice_fusion.11), channel_id=1, source_target_pairs={{0,1},{2,3},{4,5},{6,7},{8,9},{10,11},{12,13},{14,15},{16,17},{18,... | collective-permute-start | bytes 10223624 | tf_op jit(solution)/shard_map/ppermute | solution.py:85
  183.4 73.7 %collective-permute-start.26 = (bf16[2,2,4,144,1024]{4,3,0,1,2:T(8,128)(2,1)}, bf16[2,2,4,144,1024]{4,3,0,1,2:T(8,128)(2,1)}, u32[]{:S(2)}, u32[]{:S(2)}) collective-permute-start(bf16[2,2,4,144,1024]{4,3,0,1,2:T(8,128)(2,1)} %pad_maximum_fusion.5), channel_id=1, source_target_pairs={{0,1},{2,3},{4,5},{6,7},{8,9},{10,11},{12,13},{14,15},{16,17},{18,... | collective-permute-start | bytes 14155784 | tf_op jit(solution)/shard_map/ppermute | solution.py:85
  227.9 45.0 %collective-permute-start.35 = (bf16[2,2,4,32,4608]{4,3,0,1,2:T(8,128)(2,1)}, bf16[2,2,4,32,4608]{4,3,0,1,2:T(8,128)(2,1)}, u32[]{:S(2)}, u32[]{:S(2)}) collective-permute-start(bf16[2,2,4,32,4608]{4,3,0,1,2:T(8,128)(2,1)} %pad_maximum_fusion.6), channel_id=1, source_target_pairs={{0,1},{2,3},{4,5},{6,7},{8,9},{10,11},{12,13},{14,15},{16,17},{18,... | collective-permute-start | bytes 14155784 | tf_op jit(solution)/shard_map/ppermute | solution.py:85
  233.8 55.6 %collective-permute-start.17 = (bf16[2,4,2,176,1024]{4,3,2,0,1:T(8,128)(2,1)}, bf16[2,4,2,176,1024]{4,3,2,0,1:T(8,128)(2,1)}, u32[]{:S(2)}, u32[]{:S(2)}) collective-permute-start(bf16[2,4,2,176,1024]{4,3,2,0,1:T(8,128)(2,1)} %pad_maximum_fusion.4), channel_id=1, source_target_pairs={{0,1},{2,3},{4,5},{6,7},{8,9},{10,11},{12,13},{14,15},{16,17},{18,... | collective-permute-start | bytes 17301512 | tf_op jit(solution)/shard_map/ppermute | solution.py:85
  416.4 59.3 %collective-permute-start.36 = (bf16[4,2,2,104,1024]{4,3,1,2,0:T(8,128)(2,1)}, bf16[4,2,2,104,1024]{4,3,1,2,0:T(8,128)(2,1)}, u32[]{:S(2)}, u32[]{:S(2)}) collective-permute-start(bf16[4,2,2,104,1024]{4,3,1,2,0:T(8,128)(2,1)} %bitcast.461), channel_id=1, source_target_pairs={{0,1},{2,3},{4,5},{6,7},{8,9},{10,11},{12,13},{14,15},{16,17},{18,... | collective-permute-start | bytes 10223624 | tf_op jit(solution)/shard_map/ppermute | solution.py:85
  426.6 80.1 %collective-permute-start.54 = (bf16[4,2,2,144,1024]{4,3,2,0,1:T(8,128)(2,1)}, bf16[4,2,2,144,1024]{4,3,2,0,1:T(8,128)(2,1)}, u32[]{:S(2)}, u32[]{:S(2)}) collective-permute-start(bf16[4,2,2,144,1024]{4,3,2,0,1:T(8,128)(2,1)} %bitcast.460), channel_id=1, source_target_pairs={{0,1},{2,3},{4,5},{6,7},{8,9},{10,11},{12,13},{14,15},{16,17},{18,... | collective-permute-start | bytes 14155784 | tf_op jit(solution)/shard_map/ppermute | solution.py:85
  446.7 72.0 %collective-permute-start.63 = (bf16[4,2,2,144,1024]{4,3,0,1,2:T(8,128)(2,1)}, bf16[4,2,2,144,1024]{4,3,0,1,2:T(8,128)(2,1)}, u32[]{:S(2)}, u32[]{:S(2)}) collective-permute-start(bf16[4,2,2,144,1024]{4,3,0,1,2:T(8,128)(2,1)} %bitcast.459), channel_id=1, source_target_pairs={{0,1},{2,3},{4,5},{6,7},{8,9},{10,11},{12,13},{14,15},{16,17},{18,... | collective-permute-start | bytes 14155784 | tf_op jit(solution)/shard_map/ppermute | solution.py:85
  469.7 63.0 %collective-permute-start.72 = (bf16[4,2,2,32,4608]{4,3,0,1,2:T(8,128)(2,1)}, bf16[4,2,2,32,4608]{4,3,0,1,2:T(8,128)(2,1)}, u32[]{:S(2)}, u32[]{:S(2)}) collective-permute-start(bf16[4,2,2,32,4608]{4,3,0,1,2:T(8,128)(2,1)} %bitcast.458), channel_id=1, source_target_pairs={{0,1},{2,3},{4,5},{6,7},{8,9},{10,11},{12,13},{14,15},{16,17},{18,... | collective-permute-start | bytes 14155784 | tf_op jit(solution)/shard_map/ppermute | solution.py:85
  475.7 20.5 %collective-permute-start.52 = (bf16[2,32,1024]{2,1,0:T(8,128)(2,1)S(1)}, bf16[2,32,1024]{2,1,0:T(8,128)(2,1)S(1)}, u32[]{:S(2)}, u32[]{:S(2)}) collective-permute-start(bf16[2,32,1024]{2,1,0:T(8,128)(2,1)S(1)} %fusion.63), channel_id=1, source_target_pairs={{8,0},{9,1},{10,2},{11,3},{12,4},{13,5},{14,6},{15,7},{16,8},{17,9... | collective-permute-start | bytes 393224 | tf_op jit(solution)/shard_map/ppermute | solution.py:142
  480.8 24.0 %collective-permute-start.37 = (bf16[2,2,104,1024]{3,2,0,1:T(8,128)(2,1)S(1)}, bf16[2,2,104,1024]{3,2,0,1:T(8,128)(2,1)S(1)}, u32[]{:S(2)}, u32[]{:S(2)}) collective-permute-start(bf16[2,2,104,1024]{3,2,0,1:T(8,128)(2,1)S(1)} %get-tuple-element.88), channel_id=1, source_target_pairs={{0,8},{1,9},{2,10},{3,11},{4,12},{5,13},{6,14},{7,15}} | collective-permute-start | bytes 2555912 | tf_op jit(solution)/shard_map/ppermute | solution.py:141
  497.8 60.5 %collective-permute-start.53 = (bf16[32,1024]{1,0:T(8,128)(2,1)}, bf16[32,1024]{1,0:T(8,128)(2,1)}, u32[]{:S(2)}, u32[]{:S(2)}) collective-permute-start(bf16[32,1024]{1,0:T(8,128)(2,1)} %dynamic-slice_bitcast_fusion.19), channel_id=1, source_target_pairs={{0,2},{1,3},{4,6},{5,7},{8,10},{9,11},{12,14},{13,15},{16,18},{17,... | collective-permute-start | bytes 196616 | tf_op jit(solution)/shard_map/ppermute | solution.py:85
  504.8 21.4 %collective-permute-start.40 = (bf16[2,2,104,1024]{3,2,0,1:T(8,128)(2,1)S(1)}, bf16[2,2,104,1024]{3,2,0,1:T(8,128)(2,1)S(1)}, u32[]{:S(2)}, u32[]{:S(2)}) collective-permute-start(bf16[2,2,104,1024]{3,2,0,1:T(8,128)(2,1)S(1)} %get-tuple-element.89), channel_id=1, source_target_pairs={{24,16},{25,17},{26,18},{27,19},{28,20},{29,21},{30,22},{31,23}} | collective-permute-start | bytes 2555912 | tf_op jit(solution)/shard_map/ppermute | solution.py:142
  506.8 22.5 %collective-permute-start.38 = (bf16[2,2,104,1024]{3,2,0,1:T(8,128)(2,1)}, bf16[2,2,104,1024]{3,2,0,1:T(8,128)(2,1)}, u32[]{:S(2)}, u32[]{:S(2)}) collective-permute-start(bf16[2,2,104,1024]{3,2,0,1:T(8,128)(2,1)} %fusion.31), channel_id=1, source_target_pairs={{0,8},{1,9},{2,10},{3,11},{4,12},{5,13},{6,14},{7,15},{8,16},{9,17... | collective-permute-start | bytes 2555912 | tf_op jit(solution)/shard_map/ppermute | solution.py:141
  518.8 61.7 %collective-permute-start.55 = (bf16[4,2,144,1024]{3,2,1,0:T(8,128)(2,1)}, bf16[4,2,144,1024]{3,2,1,0:T(8,128)(2,1)}, u32[]{:S(2)}, u32[]{:S(2)}) collective-permute-start(bf16[4,2,144,1024]{3,2,1,0:T(8,128)(2,1)} %dynamic-slice_bitcast_fusion.2), channel_id=1, source_target_pairs={{0,4},{1,5},{2,6},{3,7},{8,12},{9,13},{10,14},{11,15},{16,20},{17,... | collective-permute-start | bytes 7077896 | tf_op jit(solution)/shard_map/ppermute | solution.py:85
  526.3 60.9 %collective-permute-start.64 = (bf16[4,2,144,1024]{3,2,0,1:T(8,128)(2,1)}, bf16[4,2,144,1024]{3,2,0,1:T(8,128)(2,1)}, u32[]{:S(2)}, u32[]{:S(2)}) collective-permute-start(bf16[4,2,144,1024]{3,2,0,1:T(8,128)(2,1)} %dynamic-slice_bitcast_fusion.1), channel_id=1, source_target_pairs={{0,2},{1,3},{4,6},{5,7},{8,10},{9,11},{12,14},{13,15},{16,18},{17,... | collective-permute-start | bytes 7077896 | tf_op jit(solution)/shard_map/ppermute | solution.py:85
  538.2 93.0 %collective-permute-start.73 = (bf16[4,2,32,4608]{3,2,0,1:T(8,128)(2,1)S(1)}, bf16[4,2,32,4608]{3,2,0,1:T(8,128)(2,1)S(1)}, u32[]{:S(2)}, u32[]{:S(2)}) collective-permute-start(bf16[4,2,32,4608]{3,2,0,1:T(8,128)(2,1)S(1)} %dynamic-slice_bitcast_fusion), channel_id=1, source_target_pairs={{0,2},{1,3},{4,6},{5,7},{8,10},{9,11},{12,14},{13,15},{16,18},{17,... | collective-permute-start | bytes 7077896 | tf_op jit(solution)/shard_map/ppermute | solution.py:85
  539.8 34.0 %collective-permute-start.39 = (bf16[2,2,104,1024]{3,2,0,1:T(8,128)(2,1)S(1)}, bf16[2,2,104,1024]{3,2,0,1:T(8,128)(2,1)S(1)}, u32[]{:S(2)}, u32[]{:S(2)}) collective-permute-start(bf16[2,2,104,1024]{3,2,0,1:T(8,128)(2,1)S(1)} %get-tuple-element.86), channel_id=1, source_target_pairs={{0,8},{1,9},{2,10},{3,11},{4,12},{5,13},{6,14},{7,15},{8,16},{9,17... | collective-permute-start | bytes 2555912 | tf_op jit(solution)/shard_map/ppermute | solution.py:141
  558.2 20.1 %collective-permute-start.42 = (bf16[2,2,104,1024]{3,2,0,1:T(8,128)(2,1)S(1)}, bf16[2,2,104,1024]{3,2,0,1:T(8,128)(2,1)S(1)}, u32[]{:S(2)}, u32[]{:S(2)}) collective-permute-start(bf16[2,2,104,1024]{3,2,0,1:T(8,128)(2,1)S(1)} %fusion.30), channel_id=1, source_target_pairs={{8,0},{9,1},{10,2},{11,3},{12,4},{13,5},{14,6},{15,7},{16,8},{17,9... | collective-permute-start | bytes 2555912 | tf_op jit(solution)/shard_map/ppermute | solution.py:142
  578.9 59.3 %collective-permute-start.43 = (bf16[2,104,1024]{2,1,0:T(8,128)(2,1)S(1)}, bf16[2,104,1024]{2,1,0:T(8,128)(2,1)S(1)}, u32[]{:S(2)}, u32[]{:S(2)}) collective-permute-start(bf16[2,104,1024]{2,1,0:T(8,128)(2,1)S(1)} %dynamic-slice_bitcast_fusion.10), channel_id=1, source_target_pairs={{0,2},{1,3},{4,6},{5,7},{8,10},{9,11},{12,14},{13,15},{16,18},{17,... | collective-permute-start | bytes 1277960 | tf_op jit(solution)/shard_map/ppermute | solution.py:85
  583.4 87.3 %collective-permute-start.56 = (bf16[2,144,1024]{2,1,0:T(8,128)(2,1)S(1)}, bf16[2,144,1024]{2,1,0:T(8,128)(2,1)S(1)}, u32[]{:S(2)}, u32[]{:S(2)}) collective-permute-start(bf16[2,144,1024]{2,1,0:T(8,128)(2,1)S(1)} %get-tuple-element.92), channel_id=1, source_target_pairs={{0,8},{1,9},{2,10},{3,11},{4,12},{5,13},{6,14},{7,15}} | collective-permute-start | bytes 1769480 | tf_op jit(solution)/shard_map/ppermute | solution.py:141
  586.2 96.5 %collective-permute-start.59 = (bf16[2,144,1024]{2,1,0:T(8,128)(2,1)S(1)}, bf16[2,144,1024]{2,1,0:T(8,128)(2,1)S(1)}, u32[]{:S(2)}, u32[]{:S(2)}) collective-permute-start(bf16[2,144,1024]{2,1,0:T(8,128)(2,1)S(1)} %get-tuple-element.93), channel_id=1, source_target_pairs={{24,16},{25,17},{26,18},{27,19},{28,20},{29,21},{30,22},{31,23}} | collective-permute-start | bytes 1769480 | tf_op jit(solution)/shard_map/ppermute | solution.py:142
  590.0 59.1 %collective-permute-start.65 = (bf16[4,144,1024]{2,1,0:T(8,128)(2,1)S(1)}, bf16[4,144,1024]{2,1,0:T(8,128)(2,1)S(1)}, u32[]{:S(2)}, u32[]{:S(2)}) collective-permute-start(bf16[4,144,1024]{2,1,0:T(8,128)(2,1)S(1)} %dynamic-slice_bitcast_fusion.4), channel_id=1, source_target_pairs={{0,4},{1,5},{2,6},{3,7},{8,12},{9,13},{10,14},{11,15},{16,20},{17,... | collective-permute-start | bytes 3538952 | tf_op jit(solution)/shard_map/ppermute | solution.py:85
  639.5 29.3 %collective-permute-start.74 = (bf16[4,32,4608]{2,1,0:T(8,128)(2,1)S(1)}, bf16[4,32,4608]{2,1,0:T(8,128)(2,1)S(1)}, u32[]{:S(2)}, u32[]{:S(2)}) collective-permute-start(bf16[4,32,4608]{2,1,0:T(8,128)(2,1)S(1)} %dynamic-slice_bitcast_fusion.3), channel_id=1, source_target_pairs={{0,4},{1,5},{2,6},{3,7},{8,12},{9,13},{10,14},{11,15},{16,20},{17,... | collective-permute-start | bytes 3538952 | tf_op jit(solution)/shard_map/ppermute | solution.py:85
  649.7 23.3 %collective-permute-start.66 = (bf16[144,1024]{1,0:T(8,128)(2,1)S(1)}, bf16[144,1024]{1,0:T(8,128)(2,1)S(1)}, u32[]{:S(2)}, u32[]{:S(2)}) collective-permute-start(bf16[144,1024]{1,0:T(8,128)(2,1)S(1)} %get-tuple-element.110), channel_id=1, source_target_pairs={{0,8},{1,9},{2,10},{3,11},{4,12},{5,13},{6,14},{7,15}} | collective-permute-start | bytes 884744 | tf_op jit(solution)/shard_map/ppermute | solution.py:141
  673.0 25.0 %collective-permute-start.78 = (bf16[32,4608]{1,0:T(8,128)(2,1)S(1)}, bf16[32,4608]{1,0:T(8,128)(2,1)S(1)}, u32[]{:S(2)}, u32[]{:S(2)}) collective-permute-start(bf16[32,4608]{1,0:T(8,128)(2,1)S(1)} %get-tuple-element.107), channel_id=1, source_target_pairs={{24,16},{25,17},{26,18},{27,19},{28,20},{29,21},{30,22},{31,23}} | collective-permute-start | bytes 884744 | tf_op jit(solution)/shard_map/ppermute | solution.py:142
  682.6 20.8 %collective-permute-start.76 = (bf16[32,4608]{1,0:T(8,128)(2,1)S(1)}, bf16[32,4608]{1,0:T(8,128)(2,1)S(1)}, u32[]{:S(2)}, u32[]{:S(2)}) collective-permute-start(bf16[32,4608]{1,0:T(8,128)(2,1)S(1)} %fusion.46), channel_id=1, source_target_pairs={{0,8},{1,9},{2,10},{3,11},{4,12},{5,13},{6,14},{7,15},{8,16},{9,17... | collective-permute-start | bytes 884744 | tf_op jit(solution)/shard_map/ppermute | solution.py:141
  692.0 27.9 %collective-permute-start.58 = (bf16[2,144,1024]{2,1,0:T(8,128)(2,1)S(1)}, bf16[2,144,1024]{2,1,0:T(8,128)(2,1)S(1)}, u32[]{:S(2)}, u32[]{:S(2)}) collective-permute-start(bf16[2,144,1024]{2,1,0:T(8,128)(2,1)S(1)} %get-tuple-element.90), channel_id=1, source_target_pairs={{0,8},{1,9},{2,10},{3,11},{4,12},{5,13},{6,14},{7,15},{8,16},{9,17... | collective-permute-start | bytes 1769480 | tf_op jit(solution)/shard_map/ppermute | solution.py:141
  704.5 20.7 %collective-permute-start.61 = (bf16[2,144,1024]{2,1,0:T(8,128)(2,1)S(1)}, bf16[2,144,1024]{2,1,0:T(8,128)(2,1)S(1)}, u32[]{:S(2)}, u32[]{:S(2)}) collective-permute-start(bf16[2,144,1024]{2,1,0:T(8,128)(2,1)S(1)} %fusion.35), channel_id=1, source_target_pairs={{8,0},{9,1},{10,2},{11,3},{12,4},{13,5},{14,6},{15,7},{16,8},{17,9... | collective-permute-start | bytes 1769480 | tf_op jit(solution)/shard_map/ppermute | solution.py:142
  705.8 28.2 %collective-permute-start.68 = (bf16[144,1024]{1,0:T(8,128)(2,1)S(1)}, bf16[144,1024]{1,0:T(8,128)(2,1)S(1)}, u32[]{:S(2)}, u32[]{:S(2)}) collective-permute-start(bf16[144,1024]{1,0:T(8,128)(2,1)S(1)} %get-tuple-element.108), channel_id=1, source_target_pairs={{0,8},{1,9},{2,10},{3,11},{4,12},{5,13},{6,14},{7,15},{8,16},{9,17... | collective-permute-start | bytes 884744 | tf_op jit(solution)/shard_map/ppermute | solution.py:141
  (113 other events, 1323.7 us)
